TPU v7x, 256 devices: a whole 4x4x8 slice. The times are simulated.
256 devices in a mesh: mem: 8 (over z_hi, y), row: 32 (over x, z_lo, core).
Axes of the slice: x: 4, y: 4, z: 8 (z_hi: 2, z_lo: 4; z = z_hi * 4 + z_lo), core: 2. Of those that a mesh axis runs over, the one named last changes fastest.
Arguments:
- members: bfloat16 [128, 8, 2, 256, 512], P('mem', None, None, 'row'), may hold values from -6 to 6
- static_scale: float32 [8, 2, 256, 512], P('mem', None, 'row'), may hold values from 0.3 to 1.5
- observed: float32 [8, 2, 256, 512], P('mem', None, 'row'), may hold values from -5 to 5, as said below
- huber_class: int32 [8, 2, 256, 512], P('mem', None, 'row'), may hold values from 0 to 3
- scale_index: int32 [2, 256, 512], P(None, 'row'), may hold values from 0 to 3
Outputs:
- control: float32 [128, 2, 256, 512], P('mem', None, 'row')
- static_control: float32 [8, 2, 256, 512], P('mem', None, 'row')
- increment: float32 [8, 2, 256, 512], P('mem', None, 'row')
Inputs may be any that keep to these rules, and one draw needn't show every extreme that they name: observed departures of order one.
All inputs are finite; a program needn't handle non-finite values.
Results may differ from a plain program's by a relative error of at most 0.0035.
Values may be sent and summed in bfloat16 or wider, within the bound.
A program may use at most 64 MiB of HBM per device.

v0:
```python
import functools
import math

import jax
import jax.numpy as jnp
from jax import lax
from jax.sharding import Mesh
from jax.sharding import PartitionSpec as P

SWEEPS = 4
ITERS = 2
ROW = ("row_0", "row_1", "row_2")
MEM = ("mem_0", "mem_1")
MEM_ROW = ("mem_0", "mem_1", "row_0", "row_1", "row_2")


kappa_table = (0.06, 0.11, 0.17, 0.23)
huber_levels = (1.0, 0.5, 1.0, 2.0)


def with_halo(block, sides, width):
    for axis, dim in sides:
        count = lax.axis_size(axis)
        forward = [(i, i + 1) for i in range(count - 1)]
        backward = [(target, source) for source, target in forward]
        low = lax.ppermute(
            lax.slice_in_dim(block, block.shape[dim] - width, None, axis=dim), axis, forward
        )
        high = lax.ppermute(lax.slice_in_dim(block, 0, width, axis=dim), axis, backward)
        block = jnp.concatenate([low, block, high], axis=dim)
    return block


def from_everyone(shard, axis):
    size = lax.axis_size(axis)
    return lax.all_to_all(
        jnp.broadcast_to(shard[None], (size, *shard.shape)), axis, 0, 0, tiled=True
    )


def laid_out(blocks, dim):
    lengths = list(blocks.shape[1:])
    lengths[dim] *= blocks.shape[0]
    return jnp.moveaxis(blocks, 0, dim).reshape(lengths)


def collect(shard, axis, dim):
    blocks = from_everyone(shard, axis)
    return laid_out(blocks, dim)


def in_blocks(shard, dim, size):
    before, after = (shard.shape[:dim], shard.shape[dim + 1 :])
    return jnp.moveaxis(shard.reshape(*before, size, -1, *after), dim, 0)


def sent_and_summed(shard, axis, dim):
    blocks = in_blocks(shard, dim, lax.axis_size(axis))
    arrived = lax.all_to_all(blocks, axis, split_axis=0, concat_axis=0, tiled=True)
    return arrived.sum(axis=0)


def by_axis(shard, axes):
    return functools.reduce(lax.psum, axes, shard)


def kappa_field(scale_index):
    result = jnp.zeros(scale_index.shape, jnp.float32)
    for level_id in range(4):
        result = result + jnp.where(scale_index == level_id, kappa_table[level_id], 0.0).astype(
            jnp.float32
        )
    return result


def threshold_field(huber_class):
    result = jnp.zeros(huber_class.shape, jnp.float32)
    for level_id in range(4):
        result = result + jnp.where(huber_class == level_id, huber_levels[level_id], 0.0).astype(
            jnp.float32
        )
    return result


def laplace(padded):
    full = jnp.pad(padded, [(0, 0)] * (padded.ndim - 1) + [(1, 1)])
    centre = full[..., 1:-1, 1:-1]
    vertical = full[..., 2:, 1:-1] + full[..., :-2, 1:-1]
    sideways = full[..., 1:-1, 2:] + full[..., 1:-1, :-2]
    return vertical + sideways - 4.0 * centre


def pad_rows(field):
    return jnp.pad(field, [(0, 0)] * (field.ndim - 2) + [(1, 1), (0, 0)])


def deep_halo(field):
    return with_halo(field, ((ROW, 2),), SWEEPS)


def local(members, static_scale, observed, huber_class, scale_index):
    local_members = members.shape[0]
    rows = members.shape[3]
    ensemble_total = local_members * lax.axis_size(MEM)
    ens_coef = math.sqrt(0.7 / (ensemble_total - 1))
    stat_coef = math.sqrt(0.3)
    kappa = kappa_field(scale_index)
    threshold = threshold_field(huber_class)
    observed_mask = (huber_class > 0).astype(jnp.float32)
    wide_kappa = with_halo(kappa, ((ROW, 1),), SWEEPS)
    global_row = lax.axis_index(ROW) * rows - SWEEPS + jnp.arange(rows + 2 * SWEEPS)
    inside = ((global_row >= 0) & (global_row < rows * lax.axis_size(ROW))).astype(jnp.float32)[
        :, None
    ]

    def forward(field):
        extended = deep_halo(field)
        for sweep in range(SWEEPS):
            extended = (extended + wide_kappa * laplace(pad_rows(extended))) * inside
        return extended[:, :, SWEEPS : SWEEPS + rows]

    control = jnp.zeros((local_members,) + scale_index.shape, jnp.float32)
    static_control = jnp.zeros(static_scale.shape, jnp.float32)
    increment = jnp.zeros(static_scale.shape, jnp.float32)
    for turn in range(ITERS):
        misfit = increment - observed
        clipped = observed_mask * jnp.clip(misfit, -threshold, threshold)
        weight = observed_mask * threshold / jnp.maximum(jnp.abs(misfit), threshold)
        sent = clipped.astype(jnp.bfloat16)
        back = jnp.sum(
            members.astype(jnp.float32) * collect(sent, MEM, 0).astype(jnp.float32)[None], axis=1
        )
        static_back = stat_coef * static_scale * sent.astype(jnp.float32)
        adjoint_extended = deep_halo(jnp.concatenate([ens_coef * back, static_back], axis=0))
        for adjoint_sweep in range(SWEEPS):
            adjoint_extended = (
                adjoint_extended + laplace(pad_rows(wide_kappa * adjoint_extended))
            ) * inside
        swept = adjoint_extended[:, :, SWEEPS : SWEEPS + rows]
        grad_ens = control + swept[:local_members]
        grad_stat = static_control + swept[local_members:]
        local_norm = jnp.sum(grad_ens * grad_ens) + jnp.sum(grad_stat * grad_stat)
        smoothed = forward(jnp.concatenate([grad_ens, grad_stat], axis=0))
        spread = smoothed[:local_members].astype(jnp.bfloat16)
        static_part = stat_coef * static_scale * smoothed[local_members:]
        image = (
            sent_and_summed(
                ens_coef
                * jnp.sum(
                    members.astype(jnp.float32) * spread.astype(jnp.float32)[:, None], axis=0
                ),
                MEM,
                0,
            )
            + static_part
        )
        local_curvature = jnp.sum(weight * image * image)
        norm, curvature = (by_axis(local_norm, MEM_ROW), by_axis(local_curvature, MEM_ROW))
        step = norm / (norm + curvature)
        control = control - step * grad_ens
        static_control = static_control - step * grad_stat
        increment = increment - step * image
    return (control, static_control, increment)


def solution(mesh):
    torus = Mesh(mesh.devices.reshape(2, 4, 4, 4, 2), ("mem_0", "mem_1", "row_0", "row_1", "row_2"))
    placed = (
        P(MEM, None, None, ROW, None),
        P(MEM, None, ROW, None),
        P(MEM, None, ROW, None),
        P(MEM, None, ROW, None),
        P(None, ROW, None),
    )
    return jax.shard_map(
        local,
        mesh=torus,
        in_specs=placed,
        out_specs=(P(MEM, None, ROW, None), P(MEM, None, ROW, None), P(MEM, None, ROW, None)),
        check_vma=False,
    )
```

profile of v0, /device:TPU:1, one launch (start us, length us, event | category | flops | bytes accessed | tf_op | source)
XLA Modules:
  0.0 253.7 jit_solution(4728595765692747666)
XLA Ops:
  0.6 0.8 convert_multiply_fusion.5
  1.5 0.7 broadcast_in_dim.83
  2.1 11.6 %all-to-all-start = ((bf16[8,1,2,8,512]{4,3,2,1,0:T(8,128)(2,1)}), bf16[8,1,2,8,512]{4,3,2,1,0:T(8,128)(2,1)S(1)}, u32[]{:S(2)}, u32[]{:S(2)}) async-start(bf16[8,1,2,8,512]{4,3,2,1,0:T(8,128)(2,1)} %broadcast_in_dim.83), calls=%async_computation | async-start | bytes 262144 | tf_op jit(solution)/shard_map/all_to_all | solution.py:36
  13.8 0.8 select_add_fusion
  14.5 8.6 %all-to-all-done = bf16[8,1,2,8,512]{4,3,2,1,0:T(8,128)(2,1)S(1)} async-done(((bf16[8,1,2,8,512]{4,3,2,1,0:T(8,128)(2,1)}), bf16[8,1,2,8,512]{4,3,2,1,0:T(8,128)(2,1)S(1)}, u32[]{:S(2)}, u32[]{:S(2)}) %all-to-all-start) | async-done | bytes 131104 | tf_op jit(solution)/shard_map/all_to_all | solution.py:36
  23.1 2.1 fusion
  25.8 4.0 %collective-permute-start.1 = (f32[17,2,4,512]{3,0,2,1:T(8,128)S(1)}, f32[17,2,4,512]{3,0,2,1:T(8,128)S(1)}, u32[]{:S(2)}, u32[]{:S(2)}) collective-permute-start(f32[17,2,4,512]{3,0,2,1:T(8,128)S(1)} %copy.27), channel_id=1, source_target_pairs={{1,0},{2,1},{3,2},{4,3},{5,4},{6,5},{7,6},{8,7},{9,8},{10,9},{11,1... | collective-permute-start | bytes 835592 | tf_op jit(solution)/shard_map/ppermute | solution.py:29
  29.8 2.7 %collective-permute-start = (f32[17,2,4,512]{3,0,2,1:T(8,128)S(1)}, f32[17,2,4,512]{3,0,2,1:T(8,128)S(1)}, u32[]{:S(2)}, u32[]{:S(2)}) collective-permute-start(f32[17,2,4,512]{3,0,2,1:T(8,128)S(1)} %copy.26), channel_id=1, source_target_pairs={{0,1},{1,2},{2,3},{3,4},{4,5},{5,6},{6,7},{7,8},{8,9},{9,10},{10,1... | collective-permute-start | bytes 835592 | tf_op jit(solution)/shard_map/ppermute | solution.py:26
  32.6 2.4 collective-permute-start.2
  35.0 1.9 collective-permute-start.3
  37.4 3.9 %collective-permute-done.3 = f32[2,4,512]{2,1,0:T(4,128)S(1)} collective-permute-done((f32[2,4,512]{2,1,0:T(4,128)S(1)}, f32[2,4,512]{2,1,0:T(4,128)S(1)}, u32[]{:S(2)}, u32[]{:S(2)}) %collective-permute-start.3) | collective-permute-done | bytes 16416 | tf_op jit(solution)/shard_map/ppermute | solution.py:29
  42.3 1.1 broadcast_multiply_fusion.5
  43.7 1.0 broadcast_multiply_fusion.4
  45.0 1.0 broadcast_multiply_fusion.3
  46.2 0.9 fusion.23
  47.4 1.9 collective-permute-start.5
  49.5 3.8 %collective-permute-start.4 = (f32[17,2,4,512]{3,0,2,1:T(8,128)S(1)}, f32[17,2,4,512]{3,0,2,1:T(8,128)S(1)}, u32[]{:S(2)}, u32[]{:S(2)}) collective-permute-start(f32[17,2,4,512]{3,0,2,1:T(8,128)S(1)} %copy.30), channel_id=1, source_target_pairs={{0,1},{1,2},{2,3},{3,4},{4,5},{5,6},{6,7},{7,8},{8,9},{9,10},{10,1... | collective-permute-start | bytes 835592 | tf_op jit(solution)/shard_map/ppermute | solution.py:26
  53.4 3.1 %collective-permute-done.5 = f32[17,2,4,512]{3,0,2,1:T(8,128)S(1)} collective-permute-done((f32[17,2,4,512]{3,0,2,1:T(8,128)S(1)}, f32[17,2,4,512]{3,0,2,1:T(8,128)S(1)}, u32[]{:S(2)}, u32[]{:S(2)}) %collective-permute-start.5) | collective-permute-done | bytes 278560 | tf_op jit(solution)/shard_map/ppermute | solution.py:29
  56.7 1.2 collective-permute-done.4
  58.5 1.0 fusion.29
  59.8 0.8 fusion.35
  60.9 0.8 fusion.41
  62.0 0.8 fusion.47
  63.0 0.6 copy-done
  64.1 0.7 multiply_bitcast_fusion.1
  64.8 3.4 %all-to-all-start.1 = ((f32[8,1,2,8,512]{4,3,2,1,0:T(8,128)}), f32[8,1,2,8,512]{4,3,2,1,0:T(8,128)S(1)}, u32[]{:S(2)}, u32[]{:S(2)}) async-start(f32[8,1,2,8,512]{4,3,2,1,0:T(8,128)} %multiply_bitcast_fusion.1), calls=%async_computation.1 | async-start | bytes 524288 | tf_op jit(solution)/shard_map/all_to_all | solution.py:59
  68.9 0.7 multiply_reduce_fusion.1
  70.9 7.3 %all-to-all-done.1 = f32[8,1,2,8,512]{4,3,2,1,0:T(8,128)S(1)} async-done(((f32[8,1,2,8,512]{4,3,2,1,0:T(8,128)}), f32[8,1,2,8,512]{4,3,2,1,0:T(8,128)S(1)}, u32[]{:S(2)}, u32[]{:S(2)}) %all-to-all-start.1) | async-done | bytes 262176 | tf_op jit(solution)/shard_map/all_to_all | solution.py:59
  78.2 0.6 reduce_sum.116
  78.8 1.5 fusion.99
  80.3 8.3 %all-reduce.41 = (f32[]{:T(128)}, f32[]{:T(128)}) all-reduce(f32[]{:T(128)S(6)} %add.381, f32[]{:T(128)} %get-tuple-element.38), channel_id=1, replica_groups=mesh['mem_0'=2,'mem_1'=4,'row_0'=4,'row_1'=4,'row_2'=2] {'mem_0'}, use_global_device_ids=true, to_apply=%region_3.4 | all-reduce | flops 2 | bytes 16 | tf_op jit(solution)/shard_map/psum | solution.py:64
  88.6 7.1 %all-reduce.37 = (f32[]{:T(128)}, f32[]{:T(128)}) all-reduce(f32[]{:T(128)} %get-tuple-element.24, f32[]{:T(128)} %get-tuple-element.25), channel_id=1, replica_groups=mesh['mem_0'=2,'mem_1'=4,'row_0'=4,'row_1'=4,'row_2'=2] {'mem_1'}, use_global_device_ids=true, to_apply=%region_4.5 | all-reduce | flops 2 | bytes 16 | tf_op jit(solution)/shard_map/psum | solution.py:64
  95.8 11.3 %all-reduce.35 = (f32[]{:T(128)}, f32[]{:T(128)}) all-reduce(f32[]{:T(128)} %get-tuple-element.16, f32[]{:T(128)} %get-tuple-element.17), channel_id=1, replica_groups=mesh['mem_0'=2,'mem_1'=4,'row_0'=4,'row_1'=4,'row_2'=2] {'row_0'}, use_global_device_ids=true, to_apply=%region_5.6 | all-reduce | flops 2 | bytes 16 | tf_op jit(solution)/shard_map/psum | solution.py:64
  107.1 12.9 %all-reduce.33 = (f32[]{:T(128)}, f32[]{:T(128)}) all-reduce(f32[]{:T(128)} %get-tuple-element.12, f32[]{:T(128)} %get-tuple-element.13), channel_id=1, replica_groups=mesh['mem_0'=2,'mem_1'=4,'row_0'=4,'row_1'=4,'row_2'=2] {'row_1'}, use_global_device_ids=true, to_apply=%region_6.7 | all-reduce | flops 2 | bytes 16 | tf_op jit(solution)/shard_map/psum | solution.py:64
  119.9 11.4 %all-reduce.39 = (f32[]{:T(128)}, f32[]{:T(128)}) all-reduce(f32[]{:T(128)} %get-tuple-element.8, f32[]{:T(128)} %get-tuple-element.9), channel_id=1, replica_groups=mesh['mem_0'=2,'mem_1'=4,'row_0'=4,'row_1'=4,'row_2'=2] {'row_2'}, use_global_device_ids=true, to_apply=%region_7.8 | all-reduce | flops 2 | bytes 16 | tf_op jit(solution)/shard_map/psum | solution.py:64
  133.3 0.8 convert_multiply_fusion.4
  134.1 11.7 %all_to_all.20 = bf16[8,1,2,8,512]{4,3,2,1,0:T(8,128)(2,1)S(1)} all-to-all(bf16[8,1,2,8,512]{4,3,2,1,0:T(8,128)(2,1)S(1)} %broadcast_in_dim.90), channel_id=1, replica_groups=mesh['mem_0'=2,'mem_1'=4,'row_0'=4,'row_1'=4,'row_2'=2] {'mem_0','mem_1'}, dimensions={0} | all-to-all | bytes 262144 | tf_op jit(solution)/shard_map/all_to_all | solution.py:36
  146.7 3.6 %collective-permute-start.7 = (f32[17,2,4,512]{3,0,2,1:T(8,128)S(1)}, f32[17,2,4,512]{3,0,2,1:T(8,128)S(1)}, u32[]{:S(2)}, u32[]{:S(2)}) collective-permute-start(f32[17,2,4,512]{3,0,2,1:T(8,128)S(1)} %copy.35), channel_id=1, source_target_pairs={{1,0},{2,1},{3,2},{4,3},{5,4},{6,5},{7,6},{8,7},{9,8},{10,9},{11,1... | collective-permute-start | bytes 835592 | tf_op jit(solution)/shard_map/ppermute | solution.py:29
  150.5 4.7 %collective-permute-start.6 = (f32[17,2,4,512]{3,0,2,1:T(8,128)S(1)}, f32[17,2,4,512]{3,0,2,1:T(8,128)S(1)}, u32[]{:S(2)}, u32[]{:S(2)}) collective-permute-start(f32[17,2,4,512]{3,0,2,1:T(8,128)S(1)} %copy.34), channel_id=1, source_target_pairs={{0,1},{1,2},{2,3},{3,4},{4,5},{5,6},{6,7},{7,8},{8,9},{9,10},{10,1... | collective-permute-start | bytes 835592 | tf_op jit(solution)/shard_map/ppermute | solution.py:26
  155.3 7.3 %collective-permute-done.7 = f32[17,2,4,512]{3,0,2,1:T(8,128)S(1)} collective-permute-done((f32[17,2,4,512]{3,0,2,1:T(8,128)S(1)}, f32[17,2,4,512]{3,0,2,1:T(8,128)S(1)}, u32[]{:S(2)}, u32[]{:S(2)}) %collective-permute-start.7) | collective-permute-done | bytes 278560 | tf_op jit(solution)/shard_map/ppermute | solution.py:29
  163.5 1.1 broadcast_multiply_fusion.2
  164.9 1.0 broadcast_multiply_fusion.1
  166.1 1.0 broadcast_multiply_fusion
  167.3 0.9 fusion.67
  168.9 0.8 multiply_reduce_fusion
  170.0 1.9 collective-permute-start.9
  172.1 3.6 %collective-permute-start.8 = (f32[17,2,4,512]{3,0,2,1:T(8,128)S(1)}, f32[17,2,4,512]{3,0,2,1:T(8,128)S(1)}, u32[]{:S(2)}, u32[]{:S(2)}) collective-permute-start(f32[17,2,4,512]{3,0,2,1:T(8,128)S(1)} %copy.38), channel_id=1, source_target_pairs={{0,1},{1,2},{2,3},{3,4},{4,5},{5,6},{6,7},{7,8},{8,9},{9,10},{10,1... | collective-permute-start | bytes 835592 | tf_op jit(solution)/shard_map/ppermute | solution.py:26
  175.8 3.3 %collective-permute-done.9 = f32[17,2,4,512]{3,0,2,1:T(8,128)S(1)} collective-permute-done((f32[17,2,4,512]{3,0,2,1:T(8,128)S(1)}, f32[17,2,4,512]{3,0,2,1:T(8,128)S(1)}, u32[]{:S(2)}, u32[]{:S(2)}) %collective-permute-start.9) | collective-permute-done | bytes 278560 | tf_op jit(solution)/shard_map/ppermute | solution.py:29
  179.3 1.2 collective-permute-done.8
  181.2 1.0 fusion.73
  182.4 0.8 fusion.79
  183.6 0.8 fusion.85
  184.7 0.8 fusion.91
  186.5 0.7 multiply_bitcast_fusion
  187.2 3.4 %all-to-all-start.3 = ((f32[8,1,2,8,512]{4,3,2,1,0:T(8,128)}), f32[8,1,2,8,512]{4,3,2,1,0:T(8,128)S(1)}, u32[]{:S(2)}, u32[]{:S(2)}) async-start(f32[8,1,2,8,512]{4,3,2,1,0:T(8,128)} %multiply_bitcast_fusion), calls=%async_computation.3 | async-start | bytes 524288 | tf_op jit(solution)/shard_map/all_to_all | solution.py:59
  191.9 8.6 %all-to-all-done.3 = f32[8,1,2,8,512]{4,3,2,1,0:T(8,128)S(1)} async-done(((f32[8,1,2,8,512]{4,3,2,1,0:T(8,128)}), f32[8,1,2,8,512]{4,3,2,1,0:T(8,128)S(1)}, u32[]{:S(2)}, u32[]{:S(2)}) %all-to-all-start.3) | async-done | bytes 262176 | tf_op jit(solution)/shard_map/all_to_all | solution.py:59
  200.6 1.5 fusion.100
  202.1 8.3 %all-reduce.40 = (f32[]{:T(128)}, f32[]{:T(128)}) all-reduce(f32[]{:T(128)S(6)} %add.418, f32[]{:T(128)} %fusion.100), channel_id=1, replica_groups=mesh['mem_0'=2,'mem_1'=4,'row_0'=4,'row_1'=4,'row_2'=2] {'mem_0'}, use_global_device_ids=true, to_apply=%region_19.20 | all-reduce | flops 2 | bytes 16 | tf_op jit(solution)/shard_map/psum | solution.py:64
  210.4 7.1 %all-reduce.36 = (f32[]{:T(128)}, f32[]{:T(128)}) all-reduce(f32[]{:T(128)} %get-tuple-element.22, f32[]{:T(128)} %get-tuple-element.23), channel_id=1, replica_groups=mesh['mem_0'=2,'mem_1'=4,'row_0'=4,'row_1'=4,'row_2'=2] {'mem_1'}, use_global_device_ids=true, to_apply=%region_20.21 | all-reduce | flops 2 | bytes 16 | tf_op jit(solution)/shard_map/psum | solution.py:64
  217.5 8.6 %all-reduce.34 = (f32[]{:T(128)}, f32[]{:T(128)}) all-reduce(f32[]{:T(128)} %get-tuple-element.14, f32[]{:T(128)} %get-tuple-element.15), channel_id=1, replica_groups=mesh['mem_0'=2,'mem_1'=4,'row_0'=4,'row_1'=4,'row_2'=2] {'row_0'}, use_global_device_ids=true, to_apply=%region_21.22 | all-reduce | flops 2 | bytes 16 | tf_op jit(solution)/shard_map/psum | solution.py:64
  226.1 11.5 %all-reduce.32 = (f32[]{:T(128)}, f32[]{:T(128)}) all-reduce(f32[]{:T(128)} %get-tuple-element.10, f32[]{:T(128)} %get-tuple-element.11), channel_id=1, replica_groups=mesh['mem_0'=2,'mem_1'=4,'row_0'=4,'row_1'=4,'row_2'=2] {'row_1'}, use_global_device_ids=true, to_apply=%region_22.23 | all-reduce | flops 2 | bytes 16 | tf_op jit(solution)/shard_map/psum | solution.py:64
  237.7 11.6 %all-reduce.38 = (f32[]{:T(128)}, f32[]{:T(128)}) all-reduce(f32[]{:T(128)} %get-tuple-element.6, f32[]{:T(128)} %get-tuple-element.7), channel_id=1, replica_groups=mesh['mem_0'=2,'mem_1'=4,'row_0'=4,'row_1'=4,'row_2'=2] {'row_2'}, use_global_device_ids=true, to_apply=%region_23.24 | all-reduce | flops 2 | bytes 16 | tf_op jit(solution)/shard_map/psum | solution.py:64
  251.2 1.5 multiply_subtract_fusion.2
  252.7 1.0 multiply_subtract_fusion
  (76 shorter events, 12.5 us)
Async XLA Ops:
  2.1 21.0 %all-to-all-start = ((bf16[8,1,2,8,512]{4,3,2,1,0:T(8,128)(2,1)}), bf16[8,1,2,8,512]{4,3,2,1,0:T(8,128)(2,1)S(1)}, u32[]{:S(2)}, u32[]{:S(2)}) async-start(bf16[8,1,2,8,512]{4,3,2,1,0:T(8,128)(2,1)} %broadcast_in_dim.83), calls=%async_computation | async-start | bytes 262144 | tf_op jit(solution)/shard_map/all_to_all | solution.py:36
  25.8 15.6 %collective-permute-start.1 = (f32[17,2,4,512]{3,0,2,1:T(8,128)S(1)}, f32[17,2,4,512]{3,0,2,1:T(8,128)S(1)}, u32[]{:S(2)}, u32[]{:S(2)}) collective-permute-start(f32[17,2,4,512]{3,0,2,1:T(8,128)S(1)} %copy.27), channel_id=1, source_target_pairs={{1,0},{2,1},{3,2},{4,3},{5,4},{6,5},{7,6},{8,7},{9,8},{10,9},{11,1... | collective-permute-start | bytes 835592 | tf_op jit(solution)/shard_map/ppermute | solution.py:29
  29.8 11.8 %collective-permute-start = (f32[17,2,4,512]{3,0,2,1:T(8,128)S(1)}, f32[17,2,4,512]{3,0,2,1:T(8,128)S(1)}, u32[]{:S(2)}, u32[]{:S(2)}) collective-permute-start(f32[17,2,4,512]{3,0,2,1:T(8,128)S(1)} %copy.26), channel_id=1, source_target_pairs={{0,1},{1,2},{2,3},{3,4},{4,5},{5,6},{6,7},{7,8},{8,9},{9,10},{10,1... | collective-permute-start | bytes 835592 | tf_op jit(solution)/shard_map/ppermute | solution.py:26
  32.6 4.9 %collective-permute-start.2 = (f32[2,4,512]{2,1,0:T(4,128)S(1)}, f32[2,4,512]{2,1,0:T(4,128)S(1)}, u32[]{:S(2)}, u32[]{:S(2)}) collective-permute-start(f32[2,4,512]{2,1,0:T(4,128)S(1)} %get-tuple-element.57), channel_id=1, source_target_pairs={{0,1},{1,2},{2,3},{3,4},{4,5},{5,6},{6,7},{7,8},{8,9},{9,10},{10,1... | collective-permute-start | bytes 49160 | tf_op jit(solution)/shard_map/ppermute | solution.py:26
  35.0 6.4 %collective-permute-start.3 = (f32[2,4,512]{2,1,0:T(4,128)S(1)}, f32[2,4,512]{2,1,0:T(4,128)S(1)}, u32[]{:S(2)}, u32[]{:S(2)}) collective-permute-start(f32[2,4,512]{2,1,0:T(4,128)S(1)} %get-tuple-element.58), channel_id=1, source_target_pairs={{1,0},{2,1},{3,2},{4,3},{5,4},{6,5},{7,6},{8,7},{9,8},{10,9},{11,1... | collective-permute-start | bytes 49160 | tf_op jit(solution)/shard_map/ppermute | solution.py:29
  47.4 9.1 %collective-permute-start.5 = (f32[17,2,4,512]{3,0,2,1:T(8,128)S(1)}, f32[17,2,4,512]{3,0,2,1:T(8,128)S(1)}, u32[]{:S(2)}, u32[]{:S(2)}) collective-permute-start(f32[17,2,4,512]{3,0,2,1:T(8,128)S(1)} %copy.31), channel_id=1, source_target_pairs={{1,0},{2,1},{3,2},{4,3},{5,4},{6,5},{7,6},{8,7},{9,8},{10,9},{11,1... | collective-permute-start | bytes 835592 | tf_op jit(solution)/shard_map/ppermute | solution.py:29
  49.5 8.3 %collective-permute-start.4 = (f32[17,2,4,512]{3,0,2,1:T(8,128)S(1)}, f32[17,2,4,512]{3,0,2,1:T(8,128)S(1)}, u32[]{:S(2)}, u32[]{:S(2)}) collective-permute-start(f32[17,2,4,512]{3,0,2,1:T(8,128)S(1)} %copy.30), channel_id=1, source_target_pairs={{0,1},{1,2},{2,3},{3,4},{4,5},{5,6},{6,7},{7,8},{8,9},{9,10},{10,1... | collective-permute-start | bytes 835592 | tf_op jit(solution)/shard_map/ppermute | solution.py:26
  62.0 1.6 copy-start
  62.9 1.2 copy-start.4
  64.8 13.3 %all-to-all-start.1 = ((f32[8,1,2,8,512]{4,3,2,1,0:T(8,128)}), f32[8,1,2,8,512]{4,3,2,1,0:T(8,128)S(1)}, u32[]{:S(2)}, u32[]{:S(2)}) async-start(f32[8,1,2,8,512]{4,3,2,1,0:T(8,128)} %multiply_bitcast_fusion.1), calls=%async_computation.1 | async-start | bytes 524288 | tf_op jit(solution)/shard_map/all_to_all | solution.py:59
  146.7 15.9 %collective-permute-start.7 = (f32[17,2,4,512]{3,0,2,1:T(8,128)S(1)}, f32[17,2,4,512]{3,0,2,1:T(8,128)S(1)}, u32[]{:S(2)}, u32[]{:S(2)}) collective-permute-start(f32[17,2,4,512]{3,0,2,1:T(8,128)S(1)} %copy.35), channel_id=1, source_target_pairs={{1,0},{2,1},{3,2},{4,3},{5,4},{6,5},{7,6},{8,7},{9,8},{10,9},{11,1... | collective-permute-start | bytes 835592 | tf_op jit(solution)/shard_map/ppermute | solution.py:29
  150.5 12.3 %collective-permute-start.6 = (f32[17,2,4,512]{3,0,2,1:T(8,128)S(1)}, f32[17,2,4,512]{3,0,2,1:T(8,128)S(1)}, u32[]{:S(2)}, u32[]{:S(2)}) collective-permute-start(f32[17,2,4,512]{3,0,2,1:T(8,128)S(1)} %copy.34), channel_id=1, source_target_pairs={{0,1},{1,2},{2,3},{3,4},{4,5},{5,6},{6,7},{7,8},{8,9},{9,10},{10,1... | collective-permute-start | bytes 835592 | tf_op jit(solution)/shard_map/ppermute | solution.py:26
  169.7 11.4 %copy-start.1 = (f32[16,2,8,512]{3,2,1,0:T(8,128)}, f32[16,2,8,512]{3,2,1,0:T(8,128)S(1)}, u32[]{:S(2)}) copy-start(f32[16,2,8,512]{3,2,1,0:T(8,128)S(1)} %get-tuple-element.29) | copy-start | bytes 1572868
  170.0 9.1 %collective-permute-start.9 = (f32[17,2,4,512]{3,0,2,1:T(8,128)S(1)}, f32[17,2,4,512]{3,0,2,1:T(8,128)S(1)}, u32[]{:S(2)}, u32[]{:S(2)}) collective-permute-start(f32[17,2,4,512]{3,0,2,1:T(8,128)S(1)} %copy.39), channel_id=1, source_target_pairs={{1,0},{2,1},{3,2},{4,3},{5,4},{6,5},{7,6},{8,7},{9,8},{10,9},{11,1... | collective-permute-start | bytes 835592 | tf_op jit(solution)/shard_map/ppermute | solution.py:29
  172.1 8.3 %collective-permute-start.8 = (f32[17,2,4,512]{3,0,2,1:T(8,128)S(1)}, f32[17,2,4,512]{3,0,2,1:T(8,128)S(1)}, u32[]{:S(2)}, u32[]{:S(2)}) collective-permute-start(f32[17,2,4,512]{3,0,2,1:T(8,128)S(1)} %copy.38), channel_id=1, source_target_pairs={{0,1},{1,2},{2,3},{3,4},{4,5},{5,6},{6,7},{7,8},{8,9},{9,10},{10,1... | collective-permute-start | bytes 835592 | tf_op jit(solution)/shard_map/ppermute | solution.py:26
  185.5 1.0 copy-start.3
  186.5 14.1 %copy-start.5 = (f32[1,2,8,512]{3,2,1,0:T(8,128)S(1)}, f32[1,2,8,512]{3,2,1,0:T(8,128)}, u32[]{:S(2)}) copy-start(f32[1,2,8,512]{3,2,1,0:T(8,128)} %param.6) | copy-start | bytes 98308
  186.5 14.1 %copy-start.6 = (f32[1,2,8,512]{3,2,1,0:T(8,128)S(1)}, f32[1,2,8,512]{3,2,1,0:T(8,128)}, u32[]{:S(2)}) copy-start(f32[1,2,8,512]{3,2,1,0:T(8,128)} %param.7) | copy-start | bytes 98308
  186.5 14.1 %copy-start.7 = (s32[1,2,8,512]{3,2,1,0:T(8,128)S(1)}, s32[1,2,8,512]{3,2,1,0:T(8,128)}, u32[]{:S(2)}) copy-start(s32[1,2,8,512]{3,2,1,0:T(8,128)} %param.8) | copy-start | bytes 98308
  186.5 66.2 %copy-start.2 = (f32[16,2,8,512]{3,2,1,0:T(8,128)S(1)}, f32[16,2,8,512]{3,2,1,0:T(8,128)}, u32[]{:S(2)}) copy-start(f32[16,2,8,512]{3,2,1,0:T(8,128)} %copy-done.1) | copy-start | bytes 1572868
  187.2 13.3 %all-to-all-start.3 = ((f32[8,1,2,8,512]{4,3,2,1,0:T(8,128)}), f32[8,1,2,8,512]{4,3,2,1,0:T(8,128)S(1)}, u32[]{:S(2)}, u32[]{:S(2)}) async-start(f32[8,1,2,8,512]{4,3,2,1,0:T(8,128)} %multiply_bitcast_fusion), calls=%async_computation.3 | async-start | bytes 524288 | tf_op jit(solution)/shard_map/all_to_all | solution.py:59
where the time goes:
time: 255 us; the launch traced here: 254 us
  blocking collectives  110 us (43%)
  starting transfers between devices  49.2 us (19%)
  waiting for transfers between devices  45 us (18%)
  other arithmetic  32.6 us (13%)
  local copies, waits for them, and re-layouts  9.09 us (4%)
  between operations  7.82 us (3%)
    psum x10, blocking collectives, by_axis(): return functools.reduce(lax.psum, axes, shard)  98.2 us
    ppermute x5, waiting for transfers between devices, with_halo(): lax.ppermute(lax.slice_in_dim(block, 0, width, axis=dim), axis, backward)  17.7 us
    ppermute x5, starting transfers between devices, with_halo(): lax.ppermute(lax.slice_in_dim(block, block.shape[dim] - width, None, axis...  17.4 us
    all_to_all x2, waiting for transfers between devices, sent_and_summed(): lax.all_to_all(blocks, axis, split_axis=0, concat_axis=0, tiled=True)  15.9 us
    ppermute x5, starting transfers between devices, with_halo(): lax.ppermute(lax.slice_in_dim(block, 0, width, axis=dim), axis, backward)  13.4 us
    all_to_all x1, blocking collectives, from_everyone(): lax.all_to_all(jnp.broadcast_to(shard[None], (size, *shard.shape)), axis,...  11.7 us
    all_to_all x1, starting transfers between devices, from_everyone(): lax.all_to_all(jnp.broadcast_to(shard[None], (size, *shard.shape)), axis,...  11.6 us
    all_to_all x1, waiting for transfers between devices, from_everyone(): lax.all_to_all(jnp.broadcast_to(shard[None], (size, *shard.shape)), axis,...  8.56 us
  transfers between devices with their start and end apart: 13, of which 10 were waited for; matrix products, arithmetic and copies ran while one was open for 1% of the time, Pallas kernels for 0%

commit v1 on v0

v1 whole, which is shorter than its diff:
```python
import functools
import math

import jax
import jax.numpy as jnp
from jax import lax
from jax.experimental import pallas as pl
from jax.experimental.pallas import tpu as pltpu
from jax.sharding import PartitionSpec as P

SWEEPS = 4
ITERS = 2
KAPPAS = (0.06, 0.11, 0.17, 0.23)
LANES = 128
STAT = math.sqrt(0.3)
MESH = pl.DeviceIdType.MESH


def sideways(w):
    lane = lax.broadcasted_iota(jnp.int32, w.shape[1:], 1)[None]
    edge = jnp.zeros_like(w[:1])
    right = pltpu.roll(w, 1, 2)
    left = pltpu.roll(w, LANES - 1, 2)
    from_left = jnp.where(lane == 0, jnp.concatenate([edge, right[:-1]], 0), right)
    from_right = jnp.where(lane == LANES - 1, jnp.concatenate([left[1:], edge], 0), left)
    return from_left + from_right


def kernel(
    n_mem, n_row, ens_coef,
    members_h, scale_h, observed_h, huber_h, index_h,
    control_o, static_o, increment_o,
    members, scale, observed, huber, index,
    sent_all, send_static, static_halo, send_index, index_halo,
    kwide, knat, turned, field, send_back, back_halo,
    grad, control, spread, partial, arrived,
    stat_grad, stat_control, stat_part, image, increment, norm_acc, first, second,
    load_sem, done_sem, sent_send, sent_recv, halo_send, halo_recv, part_send, part_recv,
    small_send, small_recv,
):
    me_m = lax.axis_index("mem")
    me_r = lax.axis_index("row")
    rows = 8
    tiles = 4
    has_low = me_r > 0
    has_high = me_r < n_row - 1

    def to(m, r):
        return {"mem": m, "row": r}

    loads = [
        pltpu.make_async_copy(observed_h, observed, load_sem.at[0]),
        pltpu.make_async_copy(huber_h, huber, load_sem.at[1]),
        pltpu.make_async_copy(index_h, index, load_sem.at[2]),
        pltpu.make_async_copy(scale_h, scale, load_sem.at[3]),
    ] + [
        pltpu.make_async_copy(
            members_h.at[:, :, :, pl.ds(j * LANES, LANES)], members.at[j], load_sem.at[4 + j]
        )
        for j in range(tiles)
    ]
    for load in loads:
        load.start()

    core = lax.rem(me_r, 2)
    pair = me_r // 2
    n_first = n_mem * 2
    n_second = n_row // 2
    my_first = me_m * 2 + core

    def first_peer(d):
        other = lax.rem(my_first + d, n_first)
        return other // 2, pair * 2 + lax.rem(other, 2)

    def second_peer(d):
        return me_m, lax.rem(pair + d, n_second) * 2 + core

    barrier = pltpu.get_barrier_semaphore()
    for d in range(1, n_first):
        pl.semaphore_signal(barrier, inc=1, device_id=to(*first_peer(d)), device_id_type=MESH)
    for d in range(1, n_second):
        pl.semaphore_signal(barrier, inc=1, device_id=to(*second_peer(d)), device_id_type=MESH)
    far = jnp.where(core == 0, me_r - 1, me_r + 1)
    has_far = jnp.logical_and(far >= 0, far < n_row)

    @pl.when(has_far)
    def _():
        pl.semaphore_signal(barrier, inc=1, device_id=to(me_m, far), device_id_type=MESH)

    def lane_tile(ref, l, j):
        return ref[l, :, j * LANES:(j + 1) * LANES]

    def cutoff(l, j):
        h = lane_tile(huber, l, j)
        return jnp.where(h == 1, 0.5, jnp.where(h == 2, 1.0, jnp.where(h == 3, 2.0, 0.0))).astype(
            jnp.float32
        )

    for load in loads[:4]:
        load.wait()
    increment[...] = jnp.zeros_like(increment)
    control[...] = jnp.zeros_like(control)
    stat_control[...] = jnp.zeros_like(stat_control)
    for j in range(tiles):
        send_index[j] = jnp.concatenate(
            [lane_tile(index, 0, j), lane_tile(index, 1, j)], 0
        ).astype(jnp.float32).astype(jnp.bfloat16)

    @pl.when(jnp.logical_not(has_low))
    def _():
        index_halo[0] = jnp.full(index_halo.shape[1:], -1.0, jnp.bfloat16)
        static_halo[:, 0] = jnp.zeros_like(static_halo[:, 0])
        for it in range(ITERS):
            for l in range(2):
                back_halo[it, 0, l] = jnp.zeros_like(back_halo[it, 0, l])

    @pl.when(jnp.logical_not(has_high))
    def _():
        index_halo[1] = jnp.full(index_halo.shape[1:], -1.0, jnp.bfloat16)
        static_halo[:, 1] = jnp.zeros_like(static_halo[:, 1])
        for it in range(ITERS):
            for l in range(2):
                back_halo[it, 1, l] = jnp.zeros_like(back_halo[it, 1, l])

    def make_sent(it):
        for j in range(tiles):
            parts = []
            for l in range(2):
                cut = cutoff(l, j)
                misfit = increment[l, j] - lane_tile(observed, l, j)
                parts.append(jnp.minimum(jnp.maximum(misfit, -cut), cut))
            value = jnp.concatenate(parts, 0).astype(jnp.bfloat16)
            sent_all[it, me_m, j] = value
            wide = value.astype(jnp.float32)
            for l in range(2):
                stat = STAT * lane_tile(scale, l, j) * wide[l * rows:(l + 1) * rows]
                field_stat = stat
                image[l, j] = field_stat
            send_static[it, j] = jnp.concatenate([image[0, j], image[1, j]], 0).astype(jnp.bfloat16)

    def rowcopy(src, dst_at, slot, side):
        target = me_r + 1 if side == 0 else me_r - 1
        return pltpu.make_async_remote_copy(
            src_ref=src, dst_ref=dst_at(side), send_sem=halo_send.at[slot, side],
            recv_sem=halo_recv.at[slot, side], device_id=to(me_m, target), device_id_type=MESH,
        )

    def row_start(src, dst_at, slot):
        @pl.when(has_high)
        def _():
            rowcopy(src, dst_at, slot, 0).start()

        @pl.when(has_low)
        def _():
            rowcopy(src, dst_at, slot, 1).start()

    def row_wait(src, dst_at, slot):
        @pl.when(has_low)
        def _():
            rowcopy(src, dst_at, slot, 0).wait_recv()

        @pl.when(has_high)
        def _():
            rowcopy(src, dst_at, slot, 1).wait_recv()

    def row_wait_send(src, dst_at, slot):
        @pl.when(has_high)
        def _():
            rowcopy(src, dst_at, slot, 0).wait_send()

        @pl.when(has_low)
        def _():
            rowcopy(src, dst_at, slot, 1).wait_send()

    n_slot = 3
    index_args = (send_index, lambda side: index_halo.at[side], ITERS * n_slot)

    def static_args(it):
        return send_static.at[it], lambda side: static_halo.at[it, side], it * n_slot

    def back_args(it, l):
        return send_back.at[it, l], lambda side: back_halo.at[it, side, l], it * n_slot + 1 + l

    def gather_copy(it, d):
        return pltpu.make_async_remote_copy(
            src_ref=sent_all.at[it, me_m], dst_ref=sent_all.at[it, me_m],
            send_sem=sent_send.at[it], recv_sem=sent_recv.at[it],
            device_id=to(lax.rem(me_m + d, n_mem), me_r), device_id_type=MESH,
        )

    def part_copy(it, l, d):
        v = lax.rem(me_m + d, n_mem)
        return pltpu.make_async_remote_copy(
            src_ref=partial.at[it, l, v], dst_ref=arrived.at[it, l, me_m],
            send_sem=part_send.at[it, l], recv_sem=part_recv.at[it, l],
            device_id=to(v, me_r), device_id_type=MESH,
        )

    def first_copy(it, d):
        m, r = first_peer(d)
        return pltpu.make_async_remote_copy(
            src_ref=first.at[it, my_first], dst_ref=first.at[it, my_first],
            send_sem=small_send.at[it, 0], recv_sem=small_recv.at[it, 0],
            device_id=to(m, r), device_id_type=MESH,
        )

    def second_copy(it, d):
        m, r = second_peer(d)
        return pltpu.make_async_remote_copy(
            src_ref=second.at[it, pair], dst_ref=second.at[it, pair],
            send_sem=small_send.at[it, 1], recv_sem=small_recv.at[it, 1],
            device_id=to(m, r), device_id_type=MESH,
        )

    def bytes_wait(ref, count, sem):
        part = ref.at[pl.ds(0, count)]
        pltpu.make_async_copy(part, part, sem).wait()

    def diffuse(it, l, g):
        low_in = jnp.where(has_low, 1.0, 0.0).astype(jnp.float32)
        high_in = jnp.where(has_high, 1.0, 0.0).astype(jnp.float32)
        for sweep in range(SWEEPS):
            lo, hi = sweep, 3 * rows - sweep

            def get(row):
                u = field[l, row, g]
                return u, u * kwide[l, row]

            _, w_prev = get(lo)
            u_cur, w_cur = get(lo + 1)
            norm = jnp.zeros((8, LANES), jnp.float32)
            for row in range(lo + 1, hi - 1):
                u_next, w_next = get(row + 1)
                out = (w_prev + w_next) + sideways(w_cur) + (u_cur - 4.0 * w_cur)
                if sweep < SWEEPS - 1:
                    field[l, row, g] = out
                else:
                    out = out + control[l, row - SWEEPS, g]
                    if row < rows:
                        out = out * low_in
                    elif row >= 2 * rows:
                        out = out * high_in
                    else:
                        norm = norm + jnp.sum(out * out, axis=0)
                    grad[l, row - SWEEPS, g] = out
                w_prev, u_cur, w_cur = w_cur, u_next, w_next
        norm_acc[...] += norm
        for sweep in range(SWEEPS):
            lo, hi = SWEEPS + sweep, 3 * rows - SWEEPS - sweep

            def load(row):
                return grad[l, row - SWEEPS, g] if sweep == 0 else field[l, row, g]

            u_prev, u_cur = load(lo), load(lo + 1)
            for row in range(lo + 1, hi - 1):
                u_next = load(row + 1)
                out = u_cur + kwide[l, row] * ((u_prev + u_next) + sideways(u_cur) - 4.0 * u_cur)
                if sweep < SWEEPS - 1:
                    field[l, row, g] = out
                else:
                    out = out.astype(jnp.bfloat16).astype(jnp.float32)
                    for j in range(tiles):
                        spread[l, j, pl.ds((row - rows) * 16 + g * 8, 8), :] = out[j]
                u_prev, u_cur = u_cur, u_next

    def diffuse_static(it, l):
        halo = static_halo[it].astype(jnp.float32)
        here = slice(l * rows, (l + 1) * rows)
        u = jnp.concatenate([halo[0, :, here], image[l], halo[1, :, here]], 1)
        k = knat[l]
        grow = me_r * rows - rows + lax.broadcasted_iota(jnp.int32, (3 * rows, LANES), 0)
        inside = jnp.logical_and(grow >= 0, grow < n_row * rows)[None]
        n = 3 * rows
        for sweep in range(SWEEPS):
            w = k * u
            u = (pltpu.roll(w, 1, 1) + pltpu.roll(w, n - 1, 1)) + sideways(w) + (u - 4.0 * w)
        u = jnp.where(inside, u + stat_control[l], 0.0)
        stat_grad[l] = u
        own = u[:, rows:2 * rows]
        norm_acc[...] += jnp.sum(own * own, axis=0)
        for sweep in range(SWEEPS):
            u = u + k * (
                (pltpu.roll(u, 1, 1) + pltpu.roll(u, n - 1, 1)) + sideways(u) - 4.0 * u
            )
        for j in range(tiles):
            stat_part[l, j] = STAT * lane_tile(scale, l, j) * u[j, rows:2 * rows]

    make_sent(0)

    @pl.when(has_far)
    def _():
        pl.semaphore_wait(barrier, n_first + n_second - 1)

    @pl.when(jnp.logical_not(has_far))
    def _():
        pl.semaphore_wait(barrier, n_first + n_second - 2)

    for it in range(ITERS):
        if it > 0:
            make_sent(it)
        for d in range(1, n_mem):
            gather_copy(it, d).start()
        if it == 0:
            row_start(*index_args)
        row_start(*static_args(it))
        norm_acc[...] = jnp.zeros_like(norm_acc)
        if it == 0:
            row_wait(*index_args)
            for j in range(tiles):
                for l in range(2):
                    here = slice(l * rows, (l + 1) * rows)
                    both = index_halo[:, j].astype(jnp.float32)
                    ids = jnp.concatenate(
                        [both[0, here], lane_tile(index, l, j).astype(jnp.float32), both[1, here]],
                        0,
                    )
                    k = jnp.zeros_like(ids)
                    for i, value in enumerate(KAPPAS):
                        k = jnp.where(ids == i, value, k)
                    knat[l, j] = k
                    for row in range(3 * rows):
                        kwide[l, row, j] = jnp.broadcast_to(k[row:row + 1], (8, LANES))
            for load in loads[4:]:
                load.wait()
        bytes_wait(sent_all.at[it], n_mem - 1, sent_recv.at[it])

        @pl.loop(0, tiles)
        def _(j):
            wide = [sent_all[it, v, j].astype(jnp.float32) for v in range(n_mem)]
            for k in range(16):
                total = members[j, k, 0].astype(jnp.float32) * wide[0]
                for v in range(1, n_mem):
                    total = total + members[j, k, v].astype(jnp.float32) * wide[v]
                total = ens_coef * total
                for l in range(2):
                    turned[l, j, k * 8:(k + 1) * 8, :] = total[l * rows:(l + 1) * rows]

        for l in range(2):
            @pl.loop(0, tiles)
            def _(j):
                for r in range(rows):
                    half = [turned[l, j, pl.ds(g * 64 + r, 8, stride=8), :] for g in range(2)]
                    for g in range(2):
                        field[l, rows + r, g, j] = half[g]
                    send_back[it, l, r, j] = jnp.concatenate(half, 0).astype(jnp.bfloat16)

            row_start(*back_args(it, l))

        row_wait(*static_args(it))
        for l in range(2):
            diffuse_static(it, l)

        for l in range(2):
            row_wait(*back_args(it, l))

            @pl.loop(0, rows)
            def _(r):
                for j in range(tiles):
                    for side in range(2):
                        value = back_halo[it, side, l, r, j].astype(jnp.float32)
                        for g in range(2):
                            field[l, side * 2 * rows + r, g, j] = value[g * 8:(g + 1) * 8]

            @pl.loop(0, 2)
            def _(g):
                diffuse(it, l, g)

            @pl.loop(0, tiles // 2)
            def _(jj):
                totals = []
                for half in range(2):
                    j = jj * 2 + half
                    total = [None] * n_mem
                    for k in range(16):
                        s = spread[l, j, pl.ds(k, 8, stride=16), :]
                        for v in range(n_mem):
                            m = members[j, k, v, l * rows:(l + 1) * rows, :].astype(jnp.float32)
                            total[v] = m * s if k == 0 else total[v] + m * s
                    totals.append(total)
                for v in range(n_mem):
                    partial[it, l, v, jj] = jnp.concatenate(
                        [totals[0][v], totals[1][v]], 0
                    ).astype(jnp.bfloat16)

            for d in range(1, n_mem):
                part_copy(it, l, d).start()
            arrived[it, l, me_m] = partial[it, l, me_m]

        curv = jnp.zeros((8, LANES), jnp.float32)
        for l in range(2):
            bytes_wait(arrived.at[it, l], n_mem - 1, part_recv.at[it, l])
            total = arrived[it, l, 0].astype(jnp.float32)
            for v in range(1, n_mem):
                total = total + arrived[it, l, v].astype(jnp.float32)
            for j in range(tiles):
                part = total[j // 2, (j % 2) * 8:(j % 2) * 8 + 8]
                img = ens_coef * part + stat_part[l, j]
                image[l, j] = img
                cut = cutoff(l, j)
                misfit = increment[l, j] - lane_tile(observed, l, j)
                weight = cut / jnp.maximum(jnp.abs(misfit), jnp.where(cut == 0.0, 1.0, cut))
                curv = curv + weight * img * img

        first[it, my_first] = jnp.concatenate(
            [
                jnp.sum(norm_acc[...], axis=0, keepdims=True),
                jnp.sum(curv, axis=0, keepdims=True),
            ],
            1,
        )
        for d in range(1, n_first):
            first_copy(it, d).start()
        bytes_wait(first.at[it], n_first - 1, small_recv.at[it, 0])
        second[it, pair] = jnp.sum(first[it], axis=0)
        for d in range(1, n_second):
            second_copy(it, d).start()
        bytes_wait(second.at[it], n_second - 1, small_recv.at[it, 1])
        sums = jnp.sum(second[it], axis=0)
        norm = jnp.sum(sums[:, :LANES], axis=1, keepdims=True)
        curvature = jnp.sum(sums[:, LANES:], axis=1, keepdims=True)
        step = jnp.broadcast_to(norm / (norm + curvature), (8, LANES))

        increment[...] = increment[...] - step * image[...]
        for l in range(2):
            for j in range(tiles):
                for third in range(3):
                    here = slice(third * 8, third * 8 + 8)
                    stat_control[l, j, here] = stat_control[l, j, here] - step * stat_grad[l, j, here]
        if it < ITERS - 1:
            @pl.loop(0, 2 * rows)
            def _(row):
                for l in range(2):
                    control[l, row] = control[l, row] - step * grad[l, row]
        else:
            @pl.loop(0, tiles)
            def _(j):
                for l in range(2):
                    for r in range(rows):
                        for g in range(2):
                            spread[l, j, r * 16 + g * 8:r * 16 + g * 8 + 8, :] = (
                                control[l, SWEEPS + r, g, j] - step * grad[l, SWEEPS + r, g, j]
                            )
            for j in range(tiles):
                for l in range(2):
                    for k in range(16):
                        control_o[k, l, :, j * LANES:(j + 1) * LANES] = spread[
                            l, j, pl.ds(k, 8, stride=16), :
                        ]

    for l in range(2):
        for j in range(tiles):
            static_o[l, :, j * LANES:(j + 1) * LANES] = stat_control[l, j, rows:2 * rows]
            increment_o[l, :, j * LANES:(j + 1) * LANES] = increment[l, j]

    row_wait_send(*index_args)
    for it in range(ITERS):
        row_wait_send(*static_args(it))
        for l in range(2):
            row_wait_send(*back_args(it, l))
            bytes_wait(arrived.at[it, l], n_mem - 1, part_send.at[it, l])
        bytes_wait(sent_all.at[it], n_mem - 1, sent_send.at[it])
        bytes_wait(first.at[it], n_first - 1, small_send.at[it, 0])
        bytes_wait(second.at[it], n_second - 1, small_send.at[it, 1])


def local(n_mem, n_row, members, static_scale, observed, huber_class, scale_index):
    k, v, _, rows, cells = members.shape
    ens_coef = math.sqrt(0.7 / (k * n_mem - 1))
    f32, bf16 = jnp.float32, jnp.bfloat16
    tiles = cells // LANES
    V = pltpu.VMEM
    scratch = [
        V((tiles, k, v, 16, LANES), bf16),
        V((2, rows, cells), f32),
        V((2, rows, cells), f32),
        V((2, rows, cells), jnp.int32),
        V((2, rows, cells), jnp.int32),
        V((ITERS, n_mem, tiles, 16, LANES), bf16),
        V((ITERS, tiles, 16, LANES), bf16),
        V((ITERS, 2, tiles, 16, LANES), bf16),
        V((tiles, 16, LANES), bf16),
        V((2, tiles, 16, LANES), bf16),
        V((2, 3 * rows, tiles, 8, LANES), f32),
        V((2, tiles, 3 * rows, LANES), f32),
        V((2, tiles, k * rows, LANES), f32),
        V((2, 3 * rows, 2, tiles, 8, LANES), f32),
        V((ITERS, 2, rows, tiles, 16, LANES), bf16),
        V((ITERS, 2, 2, rows, tiles, 16, LANES), bf16),
        V((2, 2 * rows, 2, tiles, 8, LANES), f32),
        V((2, 2 * rows, 2, tiles, 8, LANES), f32),
        V((2, tiles, k * rows, LANES), f32),
        V((ITERS, 2, n_mem, tiles // 2, 16, LANES), bf16),
        V((ITERS, 2, n_mem, tiles // 2, 16, LANES), bf16),
        V((2, tiles, 3 * rows, LANES), f32),
        V((2, tiles, 3 * rows, LANES), f32),
        V((2, tiles, rows, LANES), f32),
        V((2, tiles, rows, LANES), f32),
        V((2, tiles, rows, LANES), f32),
        V((8, LANES), f32),
        V((ITERS, n_mem * 2, 1, 2 * LANES), f32),
        V((ITERS, n_row // 2, 1, 2 * LANES), f32),
        pltpu.SemaphoreType.DMA((4 + tiles,)),
        pltpu.SemaphoreType.DMA((1,)),
        pltpu.SemaphoreType.DMA((ITERS,)),
        pltpu.SemaphoreType.DMA((ITERS,)),
        pltpu.SemaphoreType.DMA((ITERS * 3 + 1, 2)),
        pltpu.SemaphoreType.DMA((ITERS * 3 + 1, 2)),
        pltpu.SemaphoreType.DMA((ITERS, 2)),
        pltpu.SemaphoreType.DMA((ITERS, 2)),
        pltpu.SemaphoreType.DMA((ITERS, 2)),
        pltpu.SemaphoreType.DMA((ITERS, 2)),
    ]
    hbm = pl.BlockSpec(memory_space=pl.ANY)
    vmem = pl.BlockSpec(memory_space=pltpu.VMEM)
    control, static_control, increment = pl.pallas_call(
        functools.partial(kernel, n_mem, n_row, ens_coef),
        out_shape=[
            jax.ShapeDtypeStruct((k, 2, rows, cells), f32),
            jax.ShapeDtypeStruct((2, rows, cells), f32),
            jax.ShapeDtypeStruct((2, rows, cells), f32),
        ],
        in_specs=[hbm] * 5,
        out_specs=[vmem] * 3,
        scratch_shapes=scratch,
        compiler_params=pltpu.CompilerParams(
            collective_id=0, has_side_effects=True, vmem_limit_bytes=40 * 1024 * 1024
        ),
    )(
        members.reshape(k, v, 2 * rows, cells),
        static_scale[0],
        observed[0],
        huber_class[0],
        scale_index,
    )
    return control, static_control[None], increment[None]


def solution(mesh):
    sizes = dict(mesh.shape)
    placed = (
        P("mem", None, None, "row", None),
        P("mem", None, "row", None),
        P("mem", None, "row", None),
        P("mem", None, "row", None),
        P(None, "row", None),
    )
    return jax.shard_map(
        functools.partial(local, sizes["mem"], sizes["row"]),
        mesh=mesh,
        in_specs=placed,
        out_specs=(P("mem", None, "row", None),) * 3,
        check_vma=False,
    )
```

time: 255 us -> 87 us (0.34)
  blocking collectives: 110 us -> 0 us
  Pallas kernels: 0 us -> 79.3 us
  starting transfers between devices: 49.2 us -> 0 us
  waiting for transfers between devices: 45 us -> 0 us
  other arithmetic: 32.6 us -> 0 us
  between operations: 7.82 us -> 0.65 us
    psum x10 -> x0, blocking collectives: 98.2 us -> none  [by_axis(): return functools.reduce(lax.psum, axes, shard)]
    pallas_call x0 -> x1, Pallas kernels: none -> 79.3 us  [local(): pl.pallas_call(functools.partial(kernel, n_mem, n_row, ens_coef), out_sha...]
    ppermute x10 -> x0, starting transfers between devices: 30.8 us -> none  [the longest x5 17.4 us: with_halo(): lax.ppermute(lax.slice_in_dim(block, block.shape[dim] - width, None, axis...]
    all_to_all x3 -> x0, waiting for transfers between devices: 24.5 us -> none  [the longest x2 15.9 us: sent_and_summed(): lax.all_to_all(blocks, axis, split_axis=0, concat_axis=0, tiled=True)]
    ppermute x10 -> x0, waiting for transfers between devices: 20.5 us -> none  [the longest x5 17.7 us: with_halo(): lax.ppermute(lax.slice_in_dim(block, 0, width, axis=dim), axis, backward)]
    mul x24 -> x0, other arithmetic: 18.5 us -> none  [the longest x8 6.91 us: forward(): extended = (extended + wide_kappa * laplace(pad_rows(extended))) * inside]
    all_to_all x3 -> x0, starting transfers between devices: 18.5 us -> none  [the longest x1 11.6 us: from_everyone(): lax.all_to_all(jnp.broadcast_to(shard[None], (size, *shard.shape)), axis,...]
    all_to_all x1 -> x0, blocking collectives: 11.7 us -> none  [from_everyone(): lax.all_to_all(jnp.broadcast_to(shard[None], (size, *shard.shape)), axis,...]
  transfers between devices with their start and end apart: 13 -> 0, of which waited for: 10 -> 0; matrix products, arithmetic and copies ran while one was open for 1% -> 0% of each run, Pallas kernels for 0% -> 0%
where the time goes in v1:
time: 87 us; the launch traced here: 86.6 us
  Pallas kernels  79.3 us (91%)
  local copies, waits for them, and re-layouts  6.64 us (8%)
    pallas_call x1, Pallas kernels, local(): pl.pallas_call(functools.partial(kernel, n_mem, n_row, ens_coef), out_sha...  79.3 us
    unnamed x13, local copies, waits for them, and re-layouts  6.64 us

profile of v1, /device:TPU:1, one launch (start us, length us, event | category | flops | bytes accessed | tf_op | source)
XLA Modules:
  0.0 86.6 jit_solution(15102494222659535195)
XLA Ops:
  0.6 0.0 copy-start
  0.6 1.6 %copy-done = bf16[16,8,2,8,512]{4,3,2,1,0:T(8,128)(2,1)S(1)} copy-done((bf16[16,8,2,8,512]{4,3,2,1,0:T(8,128)(2,1)S(1)}, bf16[16,8,2,8,512]{4,3,2,1,0:T(8,128)(2,1)}, u32[]{:S(2)}) %copy-start) | copy-done | bytes 2097176
  2.2 0.0 copy-start.1
  2.2 0.8 copy-done.1
  3.0 0.0 copy-start.2
  3.0 0.8 copy-done.2
  3.7 0.0 copy-start.3
  3.7 0.8 copy-done.3
  4.5 0.0 copy-start.4
  4.5 0.8 copy-done.4
  5.3 79.3 %shard_map.76 = (f32[16,2,8,512]{3,2,1,0:T(8,128)S(1)}, f32[2,8,512]{2,1,0:T(8,128)S(1)}, f32[2,8,512]{2,1,0:T(8,128)S(1)}) custom-call(bf16[16,8,16,512]{3,2,1,0:T(8,128)(2,1)S(1)} %bitcast.6, f32[2,8,512]{2,1,0:T(8,128)S(1)} %bitcast.7, f32[2,8,512]{2,1,0:T(8,128)S(1)} %bitcast.8, s32[2,8,512]{2,1,0:T(8,128)S(1)} %bitcast.9, s32[2,8,512]{2,1,0:T(8,128)S(1)} %copy-done.4), custom_call_target="tpu_custom_call" | custom-call | tf_op jit(solution)/shard_map/pallas_call | solution.py:515
  84.6 0.8 copy.11
  85.4 0.6 copy.12
  86.0 0.6 copy.13
Async XLA Ops:
  0.6 1.6 %copy-start = (bf16[16,8,2,8,512]{4,3,2,1,0:T(8,128)(2,1)S(1)}, bf16[16,8,2,8,512]{4,3,2,1,0:T(8,128)(2,1)}, u32[]{:S(2)}) copy-start(bf16[16,8,2,8,512]{4,3,2,1,0:T(8,128)(2,1)} %param.5) | copy-start | bytes 6291460
  2.2 0.8 copy-start.1
  3.0 0.8 copy-start.2
  3.7 0.8 copy-start.3
  4.5 0.8 copy-start.4

commit v2 on v1

--- a/solution.py
+++ b/solution.py
@@ -29,14 +29,15 @@
 def kernel(
     n_mem, n_row, ens_coef,
     members_h, scale_h, observed_h, huber_h, index_h,
-    control_o, static_o, increment_o,
+    before_o, grad_o, stat_before_o, stat_grad_o, inc_before_o, image_o, step_o,
     members, scale, observed, huber, index,
     sent_all, send_static, static_halo, send_index, index_halo,
+    obs_all, cut_all, image_all,
     kwide, knat, turned, field, send_back, back_halo,
-    grad, control, spread, partial, arrived,
-    stat_grad, stat_control, stat_part, image, increment, norm_acc, first, second,
-    load_sem, done_sem, sent_send, sent_recv, halo_send, halo_recv, part_send, part_recv,
-    small_send, small_recv,
+    grad, spread, partial, arrived,
+    stat_grad, stat_back, stat_part, image, increment, norm_acc, step_ref, first, second,
+    load_sem, sent_send, sent_recv, halo_send, halo_recv, part_send, part_recv,
+    small_send, small_recv, obs_send, obs_recv, image_send, image_recv,
 ):
     me_m = lax.axis_index("mem")
     me_r = lax.axis_index("row")
@@ -62,24 +63,30 @@
     for load in loads:
         load.start()
 
-    core = lax.rem(me_r, 2)
-    pair = me_r // 2
-    n_first = n_mem * 2
-    n_second = n_row // 2
-    my_first = me_m * 2 + core
-
-    def first_peer(d):
-        other = lax.rem(my_first + d, n_first)
-        return other // 2, pair * 2 + lax.rem(other, 2)
-
-    def second_peer(d):
-        return me_m, lax.rem(pair + d, n_second) * 2 + core
-
+    z_hi, y = me_m // 4, lax.rem(me_m, 4)
+    x, z_lo, core = me_r // 8, lax.rem(me_r // 2, 4), lax.rem(me_r, 2)
+    z = z_hi * 4 + z_lo
+
+    def device_at(dx, dy, dz, dc):
+        zz = lax.rem(z + dz, 8)
+        m = (zz // 4) * 4 + lax.rem(y + dy, 4)
+        r = lax.rem(x + dx, 4) * 8 + lax.rem(zz, 4) * 2 + lax.rem(core + dc, 2)
+        return m, r
+
+    def hops(d):
+        return -(min(d[0], 4 - d[0]) + min(d[1], 4 - d[1]) + min(d[2], 8 - d[2]))
+
+    planes = [(dx, dy, 0, dc) for dx in range(4) for dy in range(4) for dc in range(2)]
+    planes = sorted(planes[1:], key=hops)
+    along_z = sorted([(0, 0, dz, 0) for dz in range(1, 8)], key=hops)
+    same_rows = sorted([(0, dy, dz, 0) for dz in (0, 4) for dy in range(4)][1:], key=hops)
+    my_plane = (x * 4 + y) * 2 + core
+    n_first, n_second = 32, 8
+
+    greeted = sorted(set(planes + along_z + same_rows), key=hops)
     barrier = pltpu.get_barrier_semaphore()
-    for d in range(1, n_first):
-        pl.semaphore_signal(barrier, inc=1, device_id=to(*first_peer(d)), device_id_type=MESH)
-    for d in range(1, n_second):
-        pl.semaphore_signal(barrier, inc=1, device_id=to(*second_peer(d)), device_id_type=MESH)
+    for d in greeted:
+        pl.semaphore_signal(barrier, inc=1, device_id=to(*device_at(*d)), device_id_type=MESH)
     far = jnp.where(core == 0, me_r - 1, me_r + 1)
     has_far = jnp.logical_and(far >= 0, far < n_row)
 
@@ -98,9 +105,6 @@
 
     for load in loads[:4]:
         load.wait()
-    increment[...] = jnp.zeros_like(increment)
-    control[...] = jnp.zeros_like(control)
-    stat_control[...] = jnp.zeros_like(stat_control)
     for j in range(tiles):
         send_index[j] = jnp.concatenate(
             [lane_tile(index, 0, j), lane_tile(index, 1, j)], 0
@@ -122,21 +126,36 @@
             for l in range(2):
                 back_halo[it, 1, l] = jnp.zeros_like(back_halo[it, 1, l])
 
-    def make_sent(it):
+    def static_source(it):
         for j in range(tiles):
-            parts = []
+            wide = sent_all[it, me_m, j].astype(jnp.float32)
             for l in range(2):
-                cut = cutoff(l, j)
-                misfit = increment[l, j] - lane_tile(observed, l, j)
-                parts.append(jnp.minimum(jnp.maximum(misfit, -cut), cut))
-            value = jnp.concatenate(parts, 0).astype(jnp.bfloat16)
-            sent_all[it, me_m, j] = value
-            wide = value.astype(jnp.float32)
-            for l in range(2):
-                stat = STAT * lane_tile(scale, l, j) * wide[l * rows:(l + 1) * rows]
-                field_stat = stat
-                image[l, j] = field_stat
-            send_static[it, j] = jnp.concatenate([image[0, j], image[1, j]], 0).astype(jnp.bfloat16)
+                stat_back[l, j] = STAT * lane_tile(scale, l, j) * wide[l * rows:(l + 1) * rows]
+            send_static[it, j] = jnp.concatenate(
+                [stat_back[0, j], stat_back[1, j]], 0
+            ).astype(jnp.bfloat16)
+
+    def first_sent():
+        for j in range(tiles):
+            cut = jnp.concatenate([cutoff(0, j), cutoff(1, j)], 0)
+            seen = jnp.concatenate([lane_tile(observed, 0, j), lane_tile(observed, 1, j)], 0)
+            obs_all[me_m, j] = seen
+            cut_all[me_m, j] = cut.astype(jnp.bfloat16)
+            sent_all[0, me_m, j] = jnp.minimum(jnp.maximum(0.0 - seen, -cut), cut).astype(
+                jnp.bfloat16
+            )
+
+    def next_sent(it, step):
+        both = jnp.concatenate([step, step], 0)
+
+        @pl.loop(0, n_mem)
+        def _(v):
+            for j in range(tiles):
+                cut = cut_all[v, j].astype(jnp.float32)
+                misfit = 0.0 - both * image_all[v, j].astype(jnp.float32) - obs_all[v, j]
+                sent_all[it, v, j] = jnp.minimum(jnp.maximum(misfit, -cut), cut).astype(
+                    jnp.bfloat16
+                )
 
     def rowcopy(src, dst_at, slot, side):
         target = me_r + 1 if side == 0 else me_r - 1
@@ -181,36 +200,48 @@
     def back_args(it, l):
         return send_back.at[it, l], lambda side: back_halo.at[it, side, l], it * n_slot + 1 + l
 
-    def gather_copy(it, d):
+    def push(src, dst, send, recv, device):
         return pltpu.make_async_remote_copy(
-            src_ref=sent_all.at[it, me_m], dst_ref=sent_all.at[it, me_m],
-            send_sem=sent_send.at[it], recv_sem=sent_recv.at[it],
-            device_id=to(lax.rem(me_m + d, n_mem), me_r), device_id_type=MESH,
+            src_ref=src, dst_ref=dst, send_sem=send, recv_sem=recv,
+            device_id=to(*device), device_id_type=MESH,
         )
 
+    def gather_copy(ref, send, recv, d):
+        return push(ref.at[me_m], ref.at[me_m], send, recv, device_at(*d))
+
     def part_copy(it, l, d):
-        v = lax.rem(me_m + d, n_mem)
-        return pltpu.make_async_remote_copy(
-            src_ref=partial.at[it, l, v], dst_ref=arrived.at[it, l, me_m],
-            send_sem=part_send.at[it, l], recv_sem=part_recv.at[it, l],
-            device_id=to(v, me_r), device_id_type=MESH,
+        v, r = device_at(*d)
+        return push(
+            partial.at[it, l, v], arrived.at[it, l, me_m],
+            part_send.at[it, l], part_recv.at[it, l], (v, r),
         )
 
     def first_copy(it, d):
-        m, r = first_peer(d)
-        return pltpu.make_async_remote_copy(
-            src_ref=first.at[it, my_first], dst_ref=first.at[it, my_first],
-            send_sem=small_send.at[it, 0], recv_sem=small_recv.at[it, 0],
-            device_id=to(m, r), device_id_type=MESH,
-        )
+        own = first.at[it, my_plane]
+        return push(own, own, small_send.at[it, 0], small_recv.at[it, 0], device_at(*d))
 
     def second_copy(it, d):
-        m, r = second_peer(d)
-        return pltpu.make_async_remote_copy(
-            src_ref=second.at[it, pair], dst_ref=second.at[it, pair],
-            send_sem=small_send.at[it, 1], recv_sem=small_recv.at[it, 1],
-            device_id=to(m, r), device_id_type=MESH,
-        )
+        own = second.at[it, z]
+        return push(own, own, small_send.at[it, 1], small_recv.at[it, 1], device_at(*d))
+
+    across = (0, 0, 4, 0)
+    partner = lax.rem(me_m + 4, 8)
+    along_y = [(0, dy, 0, 0) for dy in (2, 1, 3)]
+
+    def obs_across():
+        return [
+            push(ref.at[me_m], ref.at[me_m], obs_send.at[i], obs_recv.at[i], device_at(*across))
+            for i, ref in enumerate((obs_all, cut_all))
+        ]
+
+    def obs_along(i, ref, slot, k):
+        return [
+            push(
+                ref.at[slot], ref.at[slot], obs_send.at[2 + 2 * i + k],
+                obs_recv.at[2 + 2 * i + k], device_at(*d),
+            )
+            for d in along_y
+        ]
 
     def bytes_wait(ref, count, sem):
         part = ref.at[pl.ds(0, count)]
@@ -235,21 +266,22 @@
                 if sweep < SWEEPS - 1:
                     field[l, row, g] = out
                 else:
-                    out = out + control[l, row - SWEEPS, g]
+                    if it > 0:
+                        out = out - step_ref[...] * grad[0, l, row - SWEEPS, g]
                     if row < rows:
                         out = out * low_in
                     elif row >= 2 * rows:
                         out = out * high_in
                     else:
                         norm = norm + jnp.sum(out * out, axis=0)
-                    grad[l, row - SWEEPS, g] = out
+                    grad[it, l, row - SWEEPS, g] = out
                 w_prev, u_cur, w_cur = w_cur, u_next, w_next
         norm_acc[...] += norm
         for sweep in range(SWEEPS):
             lo, hi = SWEEPS + sweep, 3 * rows - SWEEPS - sweep
 
             def load(row):
-                return grad[l, row - SWEEPS, g] if sweep == 0 else field[l, row, g]
+                return grad[it, l, row - SWEEPS, g] if sweep == 0 else field[l, row, g]
 
             u_prev, u_cur = load(lo), load(lo + 1)
             for row in range(lo + 1, hi - 1):
@@ -266,7 +298,7 @@
     def diffuse_static(it, l):
         halo = static_halo[it].astype(jnp.float32)
         here = slice(l * rows, (l + 1) * rows)
-        u = jnp.concatenate([halo[0, :, here], image[l], halo[1, :, here]], 1)
+        u = jnp.concatenate([halo[0, :, here], stat_back[l], halo[1, :, here]], 1)
         k = knat[l]
         grow = me_r * rows - rows + lax.broadcasted_iota(jnp.int32, (3 * rows, LANES), 0)
         inside = jnp.logical_and(grow >= 0, grow < n_row * rows)[None]
@@ -274,8 +306,10 @@
         for sweep in range(SWEEPS):
             w = k * u
             u = (pltpu.roll(w, 1, 1) + pltpu.roll(w, n - 1, 1)) + sideways(w) + (u - 4.0 * w)
-        u = jnp.where(inside, u + stat_control[l], 0.0)
-        stat_grad[l] = u
+        if it > 0:
+            u = u - step_ref[:1] * stat_grad[0, l]
+        u = jnp.where(inside, u, 0.0)
+        stat_grad[it, l] = u
         own = u[:, rows:2 * rows]
         norm_acc[...] += jnp.sum(own * own, axis=0)
         for sweep in range(SWEEPS):
@@ -285,24 +319,29 @@
         for j in range(tiles):
             stat_part[l, j] = STAT * lane_tile(scale, l, j) * u[j, rows:2 * rows]
 
-    make_sent(0)
+    first_sent()
+    static_source(0)
 
     @pl.when(has_far)
     def _():
-        pl.semaphore_wait(barrier, n_first + n_second - 1)
+        pl.semaphore_wait(barrier, len(greeted) + 1)
 
     @pl.when(jnp.logical_not(has_far))
     def _():
-        pl.semaphore_wait(barrier, n_first + n_second - 2)
+        pl.semaphore_wait(barrier, len(greeted))
 
     for it in range(ITERS):
-        if it > 0:
-            make_sent(it)
-        for d in range(1, n_mem):
-            gather_copy(it, d).start()
         if it == 0:
+            for d in same_rows:
+                gather_copy(sent_all.at[0], sent_send, sent_recv, d).start()
             row_start(*index_args)
         row_start(*static_args(it))
+        if it == 0:
+            for copy in obs_across():
+                copy.start()
+            for i, ref in enumerate((obs_all, cut_all)):
+                for copy in obs_along(i, ref, me_m, 0):
+                    copy.start()
         norm_acc[...] = jnp.zeros_like(norm_acc)
         if it == 0:
             row_wait(*index_args)
@@ -322,7 +361,7 @@
                         kwide[l, row, j] = jnp.broadcast_to(k[row:row + 1], (8, LANES))
             for load in loads[4:]:
                 load.wait()
-        bytes_wait(sent_all.at[it], n_mem - 1, sent_recv.at[it])
+            bytes_wait(sent_all.at[0], n_mem - 1, sent_recv)
 
         @pl.loop(0, tiles)
         def _(j):
@@ -346,6 +385,12 @@
 
             row_start(*back_args(it, l))
 
+        if it == 0:
+            for copy in obs_across():
+                copy.wait_recv()
+            for i, ref in enumerate((obs_all, cut_all)):
+                for copy in obs_along(i, ref, partner, 1):
+                    copy.start()
         row_wait(*static_args(it))
         for l in range(2):
             diffuse_static(it, l)
@@ -382,7 +427,7 @@
                         [totals[0][v], totals[1][v]], 0
                     ).astype(jnp.bfloat16)
 
-            for d in range(1, n_mem):
+            for d in same_rows:
                 part_copy(it, l, d).start()
             arrived[it, l, me_m] = partial[it, l, me_m]
 
@@ -397,68 +442,89 @@
                 img = ens_coef * part + stat_part[l, j]
                 image[l, j] = img
                 cut = cutoff(l, j)
-                misfit = increment[l, j] - lane_tile(observed, l, j)
+                misfit = 0.0 - lane_tile(observed, l, j)
+                if it > 0:
+                    misfit = increment[l, j] + misfit
                 weight = cut / jnp.maximum(jnp.abs(misfit), jnp.where(cut == 0.0, 1.0, cut))
                 curv = curv + weight * img * img
 
-        first[it, my_first] = jnp.concatenate(
+        first[it, my_plane] = jnp.concatenate(
             [
                 jnp.sum(norm_acc[...], axis=0, keepdims=True),
                 jnp.sum(curv, axis=0, keepdims=True),
             ],
             1,
         )
-        for d in range(1, n_first):
+        for d in planes:
             first_copy(it, d).start()
+        if it == 0:
+            for j in range(tiles):
+                image_all[me_m, j] = jnp.concatenate([image[0, j], image[1, j]], 0).astype(
+                    jnp.bfloat16
+                )
+            for d in same_rows:
+                gather_copy(image_all, image_send, image_recv, d).start()
         bytes_wait(first.at[it], n_first - 1, small_recv.at[it, 0])
-        second[it, pair] = jnp.sum(first[it], axis=0)
-        for d in range(1, n_second):
+        second[it, z] = jnp.sum(first[it], axis=0)
+        for d in along_z:
             second_copy(it, d).start()
+        if it == 0:
+            for i, ref in enumerate((obs_all, cut_all)):
+                for k in range(2):
+                    bytes_wait(ref, 3, obs_recv.at[2 + 2 * i + k])
+            bytes_wait(image_all, n_mem - 1, image_recv)
+        else:
+            for n, out in enumerate((before_o, grad_o)):
+                @pl.loop(0, tiles)
+                def _(j):
+                    for l in range(2):
+                        for r in range(rows):
+                            for g in range(2):
+                                value = grad[n, l, SWEEPS + r, g, j]
+                                if n == 0:
+                                    value = 0.0 - step_ref[...] * value
+                                spread[l, j, r * 16 + g * 8:r * 16 + g * 8 + 8, :] = value
+
+                for j in range(tiles):
+                    for l in range(2):
+                        for k in range(16):
+                            out[k, l, :, j * LANES:(j + 1) * LANES] = spread[
+                                l, j, pl.ds(k, 8, stride=16), :
+                            ]
+            for l in range(2):
+                for j in range(tiles):
+                    lanes = slice(j * LANES, (j + 1) * LANES)
+                    own = slice(rows, 2 * rows)
+                    stat_before_o[l, :, lanes] = 0.0 - step_ref[...] * stat_grad[0, l, j, own]
+                    stat_grad_o[l, :, lanes] = stat_grad[1, l, j, own]
+                    inc_before_o[l, :, lanes] = increment[l, j]
+                    image_o[l, :, lanes] = image[l, j]
         bytes_wait(second.at[it], n_second - 1, small_recv.at[it, 1])
         sums = jnp.sum(second[it], axis=0)
         norm = jnp.sum(sums[:, :LANES], axis=1, keepdims=True)
         curvature = jnp.sum(sums[:, LANES:], axis=1, keepdims=True)
         step = jnp.broadcast_to(norm / (norm + curvature), (8, LANES))
-
-        increment[...] = increment[...] - step * image[...]
-        for l in range(2):
-            for j in range(tiles):
-                for third in range(3):
-                    here = slice(third * 8, third * 8 + 8)
-                    stat_control[l, j, here] = stat_control[l, j, here] - step * stat_grad[l, j, here]
-        if it < ITERS - 1:
-            @pl.loop(0, 2 * rows)
-            def _(row):
-                for l in range(2):
-                    control[l, row] = control[l, row] - step * grad[l, row]
+        if it == 0:
+            step_ref[...] = step
+            next_sent(1, step)
+            static_source(1)
+            increment[...] = 0.0 - step * image[...]
         else:
-            @pl.loop(0, tiles)
-            def _(j):
-                for l in range(2):
-                    for r in range(rows):
-                        for g in range(2):
-                            spread[l, j, r * 16 + g * 8:r * 16 + g * 8 + 8, :] = (
-                                control[l, SWEEPS + r, g, j] - step * grad[l, SWEEPS + r, g, j]
-                            )
-            for j in range(tiles):
-                for l in range(2):
-                    for k in range(16):
-                        control_o[k, l, :, j * LANES:(j + 1) * LANES] = spread[
-                            l, j, pl.ds(k, 8, stride=16), :
-                        ]
-
-    for l in range(2):
-        for j in range(tiles):
-            static_o[l, :, j * LANES:(j + 1) * LANES] = stat_control[l, j, rows:2 * rows]
-            increment_o[l, :, j * LANES:(j + 1) * LANES] = increment[l, j]
+            step_o[...] = step
 
     row_wait_send(*index_args)
+    bytes_wait(sent_all.at[0], n_mem - 1, sent_send)
+    bytes_wait(image_all, n_mem - 1, image_send)
+    for copy in obs_across():
+        copy.wait_send()
+    for i, ref in enumerate((obs_all, cut_all)):
+        for k in range(2):
+            bytes_wait(ref, 3, obs_send.at[2 + 2 * i + k])
     for it in range(ITERS):
         row_wait_send(*static_args(it))
         for l in range(2):
             row_wait_send(*back_args(it, l))
             bytes_wait(arrived.at[it, l], n_mem - 1, part_send.at[it, l])
-        bytes_wait(sent_all.at[it], n_mem - 1, sent_send.at[it])
         bytes_wait(first.at[it], n_first - 1, small_send.at[it, 0])
         bytes_wait(second.at[it], n_second - 1, small_send.at[it, 1])
 
@@ -480,50 +546,54 @@
         V((ITERS, 2, tiles, 16, LANES), bf16),
         V((tiles, 16, LANES), bf16),
         V((2, tiles, 16, LANES), bf16),
+        V((n_mem, tiles, 16, LANES), f32),
+        V((n_mem, tiles, 16, LANES), bf16),
+        V((n_mem, tiles, 16, LANES), bf16),
         V((2, 3 * rows, tiles, 8, LANES), f32),
         V((2, tiles, 3 * rows, LANES), f32),
         V((2, tiles, k * rows, LANES), f32),
         V((2, 3 * rows, 2, tiles, 8, LANES), f32),
         V((ITERS, 2, rows, tiles, 16, LANES), bf16),
         V((ITERS, 2, 2, rows, tiles, 16, LANES), bf16),
-        V((2, 2 * rows, 2, tiles, 8, LANES), f32),
-        V((2, 2 * rows, 2, tiles, 8, LANES), f32),
+        V((ITERS, 2, 2 * rows, 2, tiles, 8, LANES), f32),
         V((2, tiles, k * rows, LANES), f32),
         V((ITERS, 2, n_mem, tiles // 2, 16, LANES), bf16),
         V((ITERS, 2, n_mem, tiles // 2, 16, LANES), bf16),
-        V((2, tiles, 3 * rows, LANES), f32),
-        V((2, tiles, 3 * rows, LANES), f32),
+        V((ITERS, 2, tiles, 3 * rows, LANES), f32),
+        V((2, tiles, rows, LANES), f32),
         V((2, tiles, rows, LANES), f32),
         V((2, tiles, rows, LANES), f32),
         V((2, tiles, rows, LANES), f32),
         V((8, LANES), f32),
-        V((ITERS, n_mem * 2, 1, 2 * LANES), f32),
-        V((ITERS, n_row // 2, 1, 2 * LANES), f32),
+        V((8, LANES), f32),
+        V((ITERS, 32, 1, 2 * LANES), f32),
+        V((ITERS, 8, 1, 2 * LANES), f32),
         pltpu.SemaphoreType.DMA((4 + tiles,)),
-        pltpu.SemaphoreType.DMA((1,)),
-        pltpu.SemaphoreType.DMA((ITERS,)),
-        pltpu.SemaphoreType.DMA((ITERS,)),
+        pltpu.SemaphoreType.DMA,
+        pltpu.SemaphoreType.DMA,
         pltpu.SemaphoreType.DMA((ITERS * 3 + 1, 2)),
         pltpu.SemaphoreType.DMA((ITERS * 3 + 1, 2)),
         pltpu.SemaphoreType.DMA((ITERS, 2)),
         pltpu.SemaphoreType.DMA((ITERS, 2)),
         pltpu.SemaphoreType.DMA((ITERS, 2)),
         pltpu.SemaphoreType.DMA((ITERS, 2)),
+        pltpu.SemaphoreType.DMA((6,)),
+        pltpu.SemaphoreType.DMA((6,)),
+        pltpu.SemaphoreType.DMA,
+        pltpu.SemaphoreType.DMA,
     ]
-    hbm = pl.BlockSpec(memory_space=pl.ANY)
+    hbm = pl.BlockSpec(memory_space=pltpu.HBM)
     vmem = pl.BlockSpec(memory_space=pltpu.VMEM)
-    control, static_control, increment = pl.pallas_call(
+    wide = jax.ShapeDtypeStruct((k, 2, rows, cells), f32)
+    thin = jax.ShapeDtypeStruct((2, rows, cells), f32)
+    state = pl.pallas_call(
         functools.partial(kernel, n_mem, n_row, ens_coef),
-        out_shape=[
-            jax.ShapeDtypeStruct((k, 2, rows, cells), f32),
-            jax.ShapeDtypeStruct((2, rows, cells), f32),
-            jax.ShapeDtypeStruct((2, rows, cells), f32),
-        ],
+        out_shape=[wide, wide, thin, thin, thin, thin, jax.ShapeDtypeStruct((8, LANES), f32)],
         in_specs=[hbm] * 5,
-        out_specs=[vmem] * 3,
+        out_specs=[vmem] * 7,
         scratch_shapes=scratch,
         compiler_params=pltpu.CompilerParams(
-            collective_id=0, has_side_effects=True, vmem_limit_bytes=40 * 1024 * 1024
+            collective_id=0, has_side_effects=True, vmem_limit_bytes=60 * 1024 * 1024
         ),
     )(
         members.reshape(k, v, 2 * rows, cells),
@@ -532,7 +602,13 @@
         huber_class[0],
         scale_index,
     )
-    return control, static_control[None], increment[None]
+    before, grad, stat_before, stat_grad, inc_before, image, step = state
+    step = step[0, 0]
+    return (
+        before - step * grad,
+        (stat_before - step * stat_grad)[None],
+        (inc_before - step * image)[None],
+    )
 
 
 def solution(mesh):

time: 87 us -> 77.2 us (0.89)
  Pallas kernels: 79.3 us -> 70.3 us
  local copies, waits for them, and re-layouts: 6.64 us -> 1.21 us
  other arithmetic: 0 us -> 4.8 us
    pallas_call x1, Pallas kernels: 79.3 us -> 70.3 us  [local(): pl.pallas_call(functools.partial(kernel, n_mem, n_row, ens_coef), out_sha...]
    unnamed x13 -> x0, local copies, waits for them, and re-layouts: 6.64 us -> none
    sub x0 -> x1, other arithmetic: none -> 2.73 us  [local(): before - step * grad]
    broadcast_in_dim x0 -> x1, other arithmetic: none -> 2.07 us  [local(): (inc_before - step * image)[None]]
    slice x0 -> x1, local copies, waits for them, and re-layouts: none -> 1.21 us  [local(): step = step[0, 0]]
where the time goes in v2:
time: 77.2 us; the launch traced here: 76.9 us
  Pallas kernels  70.3 us (91%)
  other arithmetic  4.8 us (6%)
  local copies, waits for them, and re-layouts  1.21 us (2%)
    pallas_call x1, Pallas kernels, local(): pl.pallas_call(functools.partial(kernel, n_mem, n_row, ens_coef), out_sha...  70.3 us
    sub x1, other arithmetic, local(): before - step * grad  2.73 us
    broadcast_in_dim x1, other arithmetic, local(): (inc_before - step * image)[None]  2.07 us

profile of v2, /device:TPU:1, one launch (start us, length us, event | category | flops | bytes accessed | tf_op | source)
XLA Modules:
  0.0 76.9 jit_solution(6627003143280939716)
XLA Ops:
  0.6 70.3 %shard_map.76 = (f32[16,2,8,512]{3,2,1,0:T(8,128)}, f32[16,2,8,512]{3,2,1,0:T(8,128)}, f32[2,8,512]{2,1,0:T(8,128)}, f32[2,8,512]{2,1,0:T(8,128)}, f32[2,8,512]{...) custom-call(bf16[16,8,16,512]{3,2,1,0:T(8,128)(2,1)} %bitcast.9, f32[2,8,512]{2,1,0:T(8,128)} %bitcast.10, ...), custom_call_target="tpu_custom_call" | custom-call | tf_op jit(solution)/shard_map/pallas_call | solution.py:589
  70.9 1.2 %slice.3 = f32[1,1]{1,0:T(1,128)} slice(f32[8,128]{1,0:T(8,128)} %get-tuple-element.11), slice={[0:1], [0:1]} | slice | bytes 8 | tf_op jit(solution)/shard_map/slice | solution.py:606
  72.1 2.1 %subtract_bitcast_fusion = (f32[1,2,8,512]{3,2,1,0:T(8,128)}, f32[1,2,8,512]{3,2,1,0:T(8,128)}) fusion(f32[2,8,512]{2,1,0:T(8,128)} %get-tuple-element.15, f32[2,8,512]{2,1,0:T(8,128)} %get-tuple-element.16, f32[]{:T(128)} %bitcast.4, f32[2,8,512]{2,1,0:T(8,128)} %get-tuple-element.13, f32[2,8,512]{2,1,0:T(8,128)} %get-tuple-element.14), kind=kLoop, calls=%fused_computation.1 | loop fusion | flops 32768 | bytes 196612 | tf_op jit(solution)/shard_map/broadcast_in_dim | solution.py:610
  74.2 2.7 %multiply_subtract_fusion = f32[16,2,8,512]{3,2,1,0:T(8,128)} fusion(f32[16,2,8,512]{3,2,1,0:T(8,128)} %get-tuple-element.10, f32[16,2,8,512]{3,2,1,0:T(8,128)} %get-tuple-element.12, f32[]{:T(128)} %bitcast.4), kind=kLoop, calls=%fused_computation | loop fusion | flops 262144 | bytes 1572868 | tf_op jit(solution)/shard_map/sub | solution.py:608

commit v3 on v2

--- a/solution.py
+++ b/solution.py
@@ -584,11 +584,11 @@
     ]
     hbm = pl.BlockSpec(memory_space=pltpu.HBM)
     vmem = pl.BlockSpec(memory_space=pltpu.VMEM)
-    wide = jax.ShapeDtypeStruct((k, 2, rows, cells), f32)
-    thin = jax.ShapeDtypeStruct((2, rows, cells), f32)
+    wide = pltpu.VMEM((k, 2, rows, cells), f32)
+    thin = pltpu.VMEM((2, rows, cells), f32)
     state = pl.pallas_call(
         functools.partial(kernel, n_mem, n_row, ens_coef),
-        out_shape=[wide, wide, thin, thin, thin, thin, jax.ShapeDtypeStruct((8, LANES), f32)],
+        out_shape=[wide, wide, thin, thin, thin, thin, pltpu.VMEM((8, LANES), f32)],
         in_specs=[hbm] * 5,
         out_specs=[vmem] * 7,
         scratch_shapes=scratch,

time: 77.2 us -> 73.4 us (0.951)
  other arithmetic: 4.8 us -> 2.79 us
  Pallas kernels: 70.3 us -> 69.3 us
    sub x1, other arithmetic: 2.73 us -> 1.53 us  [local(): before - step * grad]
    pallas_call x1, Pallas kernels: 70.3 us -> 69.3 us  [local(): pl.pallas_call(functools.partial(kernel, n_mem, n_row, ens_coef), out_sha...]
    broadcast_in_dim x1, other arithmetic: 2.07 us -> 1.27 us  [local(): (inc_before - step * image)[None]]
where the time goes in v3:
time: 73.4 us; the launch traced here: 73.2 us
  Pallas kernels  69.3 us (94%)
  other arithmetic  2.79 us (4%)
    pallas_call x1, Pallas kernels, local(): pl.pallas_call(functools.partial(kernel, n_mem, n_row, ens_coef), out_sha...  69.3 us
    sub x1, other arithmetic, local(): before - step * grad  1.53 us

profile of v3, /device:TPU:1, one launch (start us, length us, event | category | flops | bytes accessed | tf_op | source)
XLA Modules:
  0.0 73.2 jit_solution(1948152468744163689)
XLA Ops:
  0.6 69.3 %shard_map.76 = (f32[16,2,8,512]{3,2,1,0:T(8,128)S(1)}, f32[16,2,8,512]{3,2,1,0:T(8,128)S(1)}, f32[2,8,512]{2,1,0:T(8,128)S(1)}, f32[2,8,512]{2,1,0:T(8,128)S(1)...) custom-call(bf16[16,8,16,512]{3,2,1,0:T(8,128)(2,1)} %bitcast.9, ...), custom_call_target="tpu_custom_call" | custom-call | tf_op jit(solution)/shard_map/pallas_call | solution.py:589
  69.9 0.5 slice.3
  70.4 1.3 %subtract_bitcast_fusion = (f32[1,2,8,512]{3,2,1,0:T(8,128)}, f32[1,2,8,512]{3,2,1,0:T(8,128)}) fusion(f32[2,8,512]{2,1,0:T(8,128)S(1)} %get-tuple-element.15, f32[2,8,512]{2,1,0:T(8,128)S(1)} %get-tuple-element.16, f32[]{:T(128)} %bitcast.4, f32[2,8,512]{2,1,0:T(8,128)S(1)} %get-tuple-element.13, f32[2,8,512]{2,1,0:T(8,128)S(1)} %get-tuple-element.14), kind=kLoop, calls=%fused_computation.1 | loop fusion | flops 32768 | bytes 196612 | tf_op jit(solution)/shard_map/broadcast_in_dim | solution.py:610
  71.7 1.5 %multiply_subtract_fusion = f32[16,2,8,512]{3,2,1,0:T(8,128)} fusion(f32[16,2,8,512]{3,2,1,0:T(8,128)S(1)} %get-tuple-element.10, f32[16,2,8,512]{3,2,1,0:T(8,128)S(1)} %get-tuple-element.12, f32[]{:T(128)} %bitcast.4), kind=kLoop, calls=%fused_computation | loop fusion | flops 262144 | bytes 1572868 | tf_op jit(solution)/shard_map/sub | solution.py:608

commit v4 on v3

--- a/solution.py
+++ b/solution.py
@@ -29,7 +29,7 @@
 def kernel(
     n_mem, n_row, ens_coef,
     members_h, scale_h, observed_h, huber_h, index_h,
-    before_o, grad_o, stat_before_o, stat_grad_o, inc_before_o, image_o, step_o,
+    control_o, static_o, increment_o,
     members, scale, observed, huber, index,
     sent_all, send_static, static_halo, send_index, index_halo,
     obs_all, cut_all, image_all,
@@ -37,7 +37,7 @@
     grad, spread, partial, arrived,
     stat_grad, stat_back, stat_part, image, increment, norm_acc, step_ref, first, second,
     load_sem, sent_send, sent_recv, halo_send, halo_recv, part_send, part_recv,
-    small_send, small_recv, obs_send, obs_recv, image_send, image_recv,
+    grad_nat, small_send, small_recv, obs_send, obs_recv, image_send, image_recv,
 ):
     me_m = lax.axis_index("mem")
     me_r = lax.axis_index("row")
@@ -116,7 +116,8 @@
         static_halo[:, 0] = jnp.zeros_like(static_halo[:, 0])
         for it in range(ITERS):
             for l in range(2):
-                back_halo[it, 0, l] = jnp.zeros_like(back_halo[it, 0, l])
+                for g in range(2):
+                    back_halo[it, 0, l, g] = jnp.zeros_like(back_halo[it, 0, l, g])
 
     @pl.when(jnp.logical_not(has_high))
     def _():
@@ -124,7 +125,8 @@
         static_halo[:, 1] = jnp.zeros_like(static_halo[:, 1])
         for it in range(ITERS):
             for l in range(2):
-                back_halo[it, 1, l] = jnp.zeros_like(back_halo[it, 1, l])
+                for g in range(2):
+                    back_halo[it, 1, l, g] = jnp.zeros_like(back_halo[it, 1, l, g])
 
     def static_source(it):
         for j in range(tiles):
@@ -191,14 +193,15 @@
         def _():
             rowcopy(src, dst_at, slot, 1).wait_send()
 
-    n_slot = 3
+    n_slot = 5
     index_args = (send_index, lambda side: index_halo.at[side], ITERS * n_slot)
 
     def static_args(it):
         return send_static.at[it], lambda side: static_halo.at[it, side], it * n_slot
 
-    def back_args(it, l):
-        return send_back.at[it, l], lambda side: back_halo.at[it, side, l], it * n_slot + 1 + l
+    def back_args(it, l, g):
+        slot = it * n_slot + 1 + g * 2 + l
+        return send_back.at[it, l, g], lambda side: back_halo.at[it, side, l, g], slot
 
     def push(src, dst, send, recv, device):
         return pltpu.make_async_remote_copy(
@@ -336,12 +339,6 @@
                 gather_copy(sent_all.at[0], sent_send, sent_recv, d).start()
             row_start(*index_args)
         row_start(*static_args(it))
-        if it == 0:
-            for copy in obs_across():
-                copy.start()
-            for i, ref in enumerate((obs_all, cut_all)):
-                for copy in obs_along(i, ref, me_m, 0):
-                    copy.start()
         norm_acc[...] = jnp.zeros_like(norm_acc)
         if it == 0:
             row_wait(*index_args)
@@ -363,52 +360,65 @@
                 load.wait()
             bytes_wait(sent_all.at[0], n_mem - 1, sent_recv)
 
-        @pl.loop(0, tiles)
-        def _(j):
-            wide = [sent_all[it, v, j].astype(jnp.float32) for v in range(n_mem)]
-            for k in range(16):
-                total = members[j, k, 0].astype(jnp.float32) * wide[0]
-                for v in range(1, n_mem):
-                    total = total + members[j, k, v].astype(jnp.float32) * wide[v]
-                total = ens_coef * total
-                for l in range(2):
-                    turned[l, j, k * 8:(k + 1) * 8, :] = total[l * rows:(l + 1) * rows]
-
-        for l in range(2):
+        for g in range(2):
             @pl.loop(0, tiles)
             def _(j):
-                for r in range(rows):
-                    half = [turned[l, j, pl.ds(g * 64 + r, 8, stride=8), :] for g in range(2)]
-                    for g in range(2):
-                        field[l, rows + r, g, j] = half[g]
-                    send_back[it, l, r, j] = jnp.concatenate(half, 0).astype(jnp.bfloat16)
-
-            row_start(*back_args(it, l))
-
-        if it == 0:
-            for copy in obs_across():
-                copy.wait_recv()
-            for i, ref in enumerate((obs_all, cut_all)):
-                for copy in obs_along(i, ref, partner, 1):
-                    copy.start()
+                wide = [sent_all[it, v, j].astype(jnp.float32) for v in range(n_mem)]
+                for k in range(g * 8, g * 8 + 8):
+                    total = members[j, k, 0].astype(jnp.float32) * wide[0]
+                    for v in range(1, n_mem):
+                        total = total + members[j, k, v].astype(jnp.float32) * wide[v]
+                    total = ens_coef * total
+                    for l in range(2):
+                        turned[l, j, k * 8:(k + 1) * 8, :] = total[l * rows:(l + 1) * rows]
+
+            for l in range(2):
+                @pl.loop(0, tiles // 2)
+                def _(jj):
+                    for r in range(rows):
+                        pair_of = [
+                            turned[l, jj * 2 + half, pl.ds(g * 64 + r, 8, stride=8), :]
+                            for half in range(2)
+                        ]
+                        for half in range(2):
+                            field[l, rows + r, g, jj * 2 + half] = pair_of[half]
+                        send_back[it, l, g, r, jj] = jnp.concatenate(pair_of, 0).astype(
+                            jnp.bfloat16
+                        )
+
+                row_start(*back_args(it, l, g))
+
         row_wait(*static_args(it))
         for l in range(2):
             diffuse_static(it, l)
 
-        for l in range(2):
-            row_wait(*back_args(it, l))
+        def arrive_and_diffuse(l, g):
+            row_wait(*back_args(it, l, g))
 
             @pl.loop(0, rows)
             def _(r):
-                for j in range(tiles):
+                for jj in range(tiles // 2):
                     for side in range(2):
-                        value = back_halo[it, side, l, r, j].astype(jnp.float32)
-                        for g in range(2):
-                            field[l, side * 2 * rows + r, g, j] = value[g * 8:(g + 1) * 8]
-
-            @pl.loop(0, 2)
-            def _(g):
-                diffuse(it, l, g)
+                        value = back_halo[it, side, l, g, r, jj].astype(jnp.float32)
+                        for half in range(2):
+                            field[l, side * 2 * rows + r, g, jj * 2 + half] = value[
+                                half * 8:(half + 1) * 8
+                            ]
+
+            diffuse(it, l, g)
+
+        @pl.loop(0, 2)
+        def _(l):
+            arrive_and_diffuse(l, 0)
+
+        for l in range(2):
+            if it == 0 and l == 1:
+                for copy in obs_across():
+                    copy.start()
+                for i, ref in enumerate((obs_all, cut_all)):
+                    for copy in obs_along(i, ref, me_m, 0):
+                        copy.start()
+            arrive_and_diffuse(l, 1)
 
             @pl.loop(0, tiles // 2)
             def _(jj):
@@ -448,6 +458,9 @@
                 weight = cut / jnp.maximum(jnp.abs(misfit), jnp.where(cut == 0.0, 1.0, cut))
                 curv = curv + weight * img * img
 
+        if it == 0:
+            for copy in obs_across():
+                copy.wait_recv()
         first[it, my_plane] = jnp.concatenate(
             [
                 jnp.sum(norm_acc[...], axis=0, keepdims=True),
@@ -464,6 +477,9 @@
                 )
             for d in same_rows:
                 gather_copy(image_all, image_send, image_recv, d).start()
+            for i, ref in enumerate((obs_all, cut_all)):
+                for copy in obs_along(i, ref, partner, 1):
+                    copy.start()
         bytes_wait(first.at[it], n_first - 1, small_recv.at[it, 0])
         second[it, z] = jnp.sum(first[it], axis=0)
         for d in along_z:
@@ -474,7 +490,7 @@
                     bytes_wait(ref, 3, obs_recv.at[2 + 2 * i + k])
             bytes_wait(image_all, n_mem - 1, image_recv)
         else:
-            for n, out in enumerate((before_o, grad_o)):
+            for n, out in enumerate((control_o, grad_nat)):
                 @pl.loop(0, tiles)
                 def _(j):
                     for l in range(2):
@@ -491,14 +507,6 @@
                             out[k, l, :, j * LANES:(j + 1) * LANES] = spread[
                                 l, j, pl.ds(k, 8, stride=16), :
                             ]
-            for l in range(2):
-                for j in range(tiles):
-                    lanes = slice(j * LANES, (j + 1) * LANES)
-                    own = slice(rows, 2 * rows)
-                    stat_before_o[l, :, lanes] = 0.0 - step_ref[...] * stat_grad[0, l, j, own]
-                    stat_grad_o[l, :, lanes] = stat_grad[1, l, j, own]
-                    inc_before_o[l, :, lanes] = increment[l, j]
-                    image_o[l, :, lanes] = image[l, j]
         bytes_wait(second.at[it], n_second - 1, small_recv.at[it, 1])
         sums = jnp.sum(second[it], axis=0)
         norm = jnp.sum(sums[:, :LANES], axis=1, keepdims=True)
@@ -510,7 +518,22 @@
             static_source(1)
             increment[...] = 0.0 - step * image[...]
         else:
-            step_o[...] = step
+            @pl.loop(0, control_o.shape[0])
+            def _(k):
+                for l in range(2):
+                    for j in range(tiles):
+                        lanes = slice(j * LANES, (j + 1) * LANES)
+                        control_o[k, l, :, lanes] = (
+                            control_o[k, l, :, lanes] - step * grad_nat[k, l, :, lanes]
+                        )
+            for l in range(2):
+                for j in range(tiles):
+                    lanes = slice(j * LANES, (j + 1) * LANES)
+                    own = slice(rows, 2 * rows)
+                    static_o[l, :, lanes] = (
+                        0.0 - step_ref[...] * stat_grad[0, l, j, own] - step * stat_grad[1, l, j, own]
+                    )
+                    increment_o[l, :, lanes] = increment[l, j] - step * image[l, j]
 
     row_wait_send(*index_args)
     bytes_wait(sent_all.at[0], n_mem - 1, sent_send)
@@ -523,7 +546,8 @@
     for it in range(ITERS):
         row_wait_send(*static_args(it))
         for l in range(2):
-            row_wait_send(*back_args(it, l))
+            for g in range(2):
+                row_wait_send(*back_args(it, l, g))
             bytes_wait(arrived.at[it, l], n_mem - 1, part_send.at[it, l])
         bytes_wait(first.at[it], n_first - 1, small_send.at[it, 0])
         bytes_wait(second.at[it], n_second - 1, small_send.at[it, 1])
@@ -553,8 +577,8 @@
         V((2, tiles, 3 * rows, LANES), f32),
         V((2, tiles, k * rows, LANES), f32),
         V((2, 3 * rows, 2, tiles, 8, LANES), f32),
-        V((ITERS, 2, rows, tiles, 16, LANES), bf16),
-        V((ITERS, 2, 2, rows, tiles, 16, LANES), bf16),
+        V((ITERS, 2, 2, rows, tiles // 2, 16, LANES), bf16),
+        V((ITERS, 2, 2, 2, rows, tiles // 2, 16, LANES), bf16),
         V((ITERS, 2, 2 * rows, 2, tiles, 8, LANES), f32),
         V((2, tiles, k * rows, LANES), f32),
         V((ITERS, 2, n_mem, tiles // 2, 16, LANES), bf16),
@@ -571,10 +595,11 @@
         pltpu.SemaphoreType.DMA((4 + tiles,)),
         pltpu.SemaphoreType.DMA,
         pltpu.SemaphoreType.DMA,
-        pltpu.SemaphoreType.DMA((ITERS * 3 + 1, 2)),
-        pltpu.SemaphoreType.DMA((ITERS * 3 + 1, 2)),
+        pltpu.SemaphoreType.DMA((ITERS * 5 + 1, 2)),
+        pltpu.SemaphoreType.DMA((ITERS * 5 + 1, 2)),
         pltpu.SemaphoreType.DMA((ITERS, 2)),
         pltpu.SemaphoreType.DMA((ITERS, 2)),
+        V((k, 2, rows, cells), f32),
         pltpu.SemaphoreType.DMA((ITERS, 2)),
         pltpu.SemaphoreType.DMA((ITERS, 2)),
         pltpu.SemaphoreType.DMA((6,)),
@@ -584,13 +609,13 @@
     ]
     hbm = pl.BlockSpec(memory_space=pltpu.HBM)
     vmem = pl.BlockSpec(memory_space=pltpu.VMEM)
-    wide = pltpu.VMEM((k, 2, rows, cells), f32)
-    thin = pltpu.VMEM((2, rows, cells), f32)
+    wide = (k, 2, rows, cells)
+    thin = (2, rows, cells)
     state = pl.pallas_call(
         functools.partial(kernel, n_mem, n_row, ens_coef),
-        out_shape=[wide, wide, thin, thin, thin, thin, pltpu.VMEM((8, LANES), f32)],
+        out_shape=[pltpu.VMEM(wide, f32), pltpu.VMEM(thin, f32), pltpu.VMEM(thin, f32)],
         in_specs=[hbm] * 5,
-        out_specs=[vmem] * 7,
+        out_specs=[vmem] * 3,
         scratch_shapes=scratch,
         compiler_params=pltpu.CompilerParams(
             collective_id=0, has_side_effects=True, vmem_limit_bytes=60 * 1024 * 1024
@@ -602,13 +627,8 @@
         huber_class[0],
         scale_index,
     )
-    before, grad, stat_before, stat_grad, inc_before, image, step = state
-    step = step[0, 0]
-    return (
-        before - step * grad,
-        (stat_before - step * stat_grad)[None],
-        (inc_before - step * image)[None],
-    )
+    control, static_control, increment = state
+    return control, static_control[None], increment[None]
 
 
 def solution(mesh):

time: 73.4 us -> 71.1 us (0.969)
  other arithmetic: 2.79 us -> 0 us
  local copies, waits for them, and re-layouts: 0.54 us -> 2.02 us
  Pallas kernels: 69.3 us -> 68.4 us
    unnamed x0 -> x3, local copies, waits for them, and re-layouts: none -> 2.02 us
    sub x1 -> x0, other arithmetic: 1.53 us -> none  [local(): before - step * grad]
    broadcast_in_dim x1 -> x0, other arithmetic: 1.27 us -> none  [local(): (inc_before - step * image)[None]]
    pallas_call x1, Pallas kernels: 69.3 us -> 68.4 us  [local(): pl.pallas_call(functools.partial(kernel, n_mem, n_row, ens_coef), out_sha...]
where the time goes in v4:
time: 71.1 us; the launch traced here: 71 us
  Pallas kernels  68.4 us (96%)
  local copies, waits for them, and re-layouts  2.02 us (3%)
    pallas_call x1, Pallas kernels, local(): pl.pallas_call(functools.partial(kernel, n_mem, n_row, ens_coef), out_sha...  68.4 us
    unnamed x3, local copies, waits for them, and re-layouts  2.02 us

profile of v4, /device:TPU:1, one launch (start us, length us, event | category | flops | bytes accessed | tf_op | source)
XLA Modules:
  0.0 71.0 jit_solution(6403467286139471011)
XLA Ops:
  0.6 68.4 %shard_map.76 = (f32[16,2,8,512]{3,2,1,0:T(8,128)S(1)}, f32[2,8,512]{2,1,0:T(8,128)S(1)}, f32[2,8,512]{2,1,0:T(8,128)S(1)}) custom-call(bf16[16,8,16,512]{3,2,1,0:T(8,128)(2,1)} %bitcast.8, f32[2,8,512]{2,1,0:T(8,128)} %bitcast.9, f32[2,8,512]{2,1,0:T(8,128)} %bitcast.10, s32[2,8,512]{2,1,0:T(8,128)} %bitcast.11, s32[2,8,512]{2,1,0:T(8,128)} %index_h.1), custom_call_target="tpu_custom_call" | custom-call | tf_op jit(solution)/shard_map/pallas_call | solution.py:614
  69.0 0.8 %copy.11 = f32[16,2,8,512]{3,2,1,0:T(8,128)} copy(f32[16,2,8,512]{3,2,1,0:T(8,128)S(1)} %get-tuple-element.9) | data formatting | bytes 1048576
  69.8 0.6 copy.12
  70.4 0.6 copy.13

commit v5 on v4

--- a/solution.py
+++ b/solution.py
@@ -32,7 +32,7 @@
     control_o, static_o, increment_o,
     members, scale, observed, huber, index,
     sent_all, send_static, static_halo, send_index, index_halo,
-    obs_all, cut_all, image_all,
+    seen_all, image_all,
     kwide, knat, turned, field, send_back, back_halo,
     grad, spread, partial, arrived,
     stat_grad, stat_back, stat_part, image, increment, norm_acc, step_ref, first, second,
@@ -141,8 +141,8 @@
         for j in range(tiles):
             cut = jnp.concatenate([cutoff(0, j), cutoff(1, j)], 0)
             seen = jnp.concatenate([lane_tile(observed, 0, j), lane_tile(observed, 1, j)], 0)
-            obs_all[me_m, j] = seen
-            cut_all[me_m, j] = cut.astype(jnp.bfloat16)
+            seen_all[me_m, j] = seen.astype(jnp.bfloat16)
+            seen_all[me_m, tiles + j] = cut.astype(jnp.bfloat16)
             sent_all[0, me_m, j] = jnp.minimum(jnp.maximum(0.0 - seen, -cut), cut).astype(
                 jnp.bfloat16
             )
@@ -153,8 +153,9 @@
         @pl.loop(0, n_mem)
         def _(v):
             for j in range(tiles):
-                cut = cut_all[v, j].astype(jnp.float32)
-                misfit = 0.0 - both * image_all[v, j].astype(jnp.float32) - obs_all[v, j]
+                cut = seen_all[v, tiles + j].astype(jnp.float32)
+                seen = seen_all[v, j].astype(jnp.float32)
+                misfit = 0.0 - both * image_all[v, j].astype(jnp.float32) - seen
                 sent_all[it, v, j] = jnp.minimum(jnp.maximum(misfit, -cut), cut).astype(
                     jnp.bfloat16
                 )
@@ -231,20 +232,13 @@
     partner = lax.rem(me_m + 4, 8)
     along_y = [(0, dy, 0, 0) for dy in (2, 1, 3)]
 
-    def obs_across():
-        return [
-            push(ref.at[me_m], ref.at[me_m], obs_send.at[i], obs_recv.at[i], device_at(*across))
-            for i, ref in enumerate((obs_all, cut_all))
-        ]
-
-    def obs_along(i, ref, slot, k):
-        return [
-            push(
-                ref.at[slot], ref.at[slot], obs_send.at[2 + 2 * i + k],
-                obs_recv.at[2 + 2 * i + k], device_at(*d),
-            )
-            for d in along_y
-        ]
+    def seen_across():
+        own = seen_all.at[me_m]
+        return push(own, own, obs_send.at[0], obs_recv.at[0], device_at(*across))
+
+    def seen_along(slot, k):
+        own = seen_all.at[slot]
+        return [push(own, own, obs_send.at[k], obs_recv.at[k], device_at(*d)) for d in along_y]
 
     def bytes_wait(ref, count, sem):
         part = ref.at[pl.ds(0, count)]
@@ -338,6 +332,7 @@
             for d in same_rows:
                 gather_copy(sent_all.at[0], sent_send, sent_recv, d).start()
             row_start(*index_args)
+            seen_across().start()
         row_start(*static_args(it))
         norm_acc[...] = jnp.zeros_like(norm_acc)
         if it == 0:
@@ -388,6 +383,12 @@
 
                 row_start(*back_args(it, l, g))
 
+        if it == 0:
+            for copy in seen_along(me_m, 1):
+                copy.start()
+            seen_across().wait_recv()
+            for copy in seen_along(partner, 2):
+                copy.start()
         row_wait(*static_args(it))
         for l in range(2):
             diffuse_static(it, l)
@@ -412,12 +413,6 @@
             arrive_and_diffuse(l, 0)
 
         for l in range(2):
-            if it == 0 and l == 1:
-                for copy in obs_across():
-                    copy.start()
-                for i, ref in enumerate((obs_all, cut_all)):
-                    for copy in obs_along(i, ref, me_m, 0):
-                        copy.start()
             arrive_and_diffuse(l, 1)
 
             @pl.loop(0, tiles // 2)
@@ -458,9 +453,6 @@
                 weight = cut / jnp.maximum(jnp.abs(misfit), jnp.where(cut == 0.0, 1.0, cut))
                 curv = curv + weight * img * img
 
-        if it == 0:
-            for copy in obs_across():
-                copy.wait_recv()
         first[it, my_plane] = jnp.concatenate(
             [
                 jnp.sum(norm_acc[...], axis=0, keepdims=True),
@@ -477,17 +469,13 @@
                 )
             for d in same_rows:
                 gather_copy(image_all, image_send, image_recv, d).start()
-            for i, ref in enumerate((obs_all, cut_all)):
-                for copy in obs_along(i, ref, partner, 1):
-                    copy.start()
         bytes_wait(first.at[it], n_first - 1, small_recv.at[it, 0])
         second[it, z] = jnp.sum(first[it], axis=0)
         for d in along_z:
             second_copy(it, d).start()
         if it == 0:
-            for i, ref in enumerate((obs_all, cut_all)):
-                for k in range(2):
-                    bytes_wait(ref, 3, obs_recv.at[2 + 2 * i + k])
+            for k in (1, 2):
+                bytes_wait(seen_all, 3, obs_recv.at[k])
             bytes_wait(image_all, n_mem - 1, image_recv)
         else:
             for n, out in enumerate((control_o, grad_nat)):
@@ -538,11 +526,9 @@
     row_wait_send(*index_args)
     bytes_wait(sent_all.at[0], n_mem - 1, sent_send)
     bytes_wait(image_all, n_mem - 1, image_send)
-    for copy in obs_across():
-        copy.wait_send()
-    for i, ref in enumerate((obs_all, cut_all)):
-        for k in range(2):
-            bytes_wait(ref, 3, obs_send.at[2 + 2 * i + k])
+    seen_across().wait_send()
+    for k in (1, 2):
+        bytes_wait(seen_all, 3, obs_send.at[k])
     for it in range(ITERS):
         row_wait_send(*static_args(it))
         for l in range(2):
@@ -570,8 +556,7 @@
         V((ITERS, 2, tiles, 16, LANES), bf16),
         V((tiles, 16, LANES), bf16),
         V((2, tiles, 16, LANES), bf16),
-        V((n_mem, tiles, 16, LANES), f32),
-        V((n_mem, tiles, 16, LANES), bf16),
+        V((n_mem, 2 * tiles, 16, LANES), bf16),
         V((n_mem, tiles, 16, LANES), bf16),
         V((2, 3 * rows, tiles, 8, LANES), f32),
         V((2, tiles, 3 * rows, LANES), f32),
@@ -602,8 +587,8 @@
         V((k, 2, rows, cells), f32),
         pltpu.SemaphoreType.DMA((ITERS, 2)),
         pltpu.SemaphoreType.DMA((ITERS, 2)),
-        pltpu.SemaphoreType.DMA((6,)),
-        pltpu.SemaphoreType.DMA((6,)),
+        pltpu.SemaphoreType.DMA((3,)),
+        pltpu.SemaphoreType.DMA((3,)),
         pltpu.SemaphoreType.DMA,
         pltpu.SemaphoreType.DMA,
     ]

time: 71.1 us -> 69.9 us (0.983)
  Pallas kernels: 68.4 us -> 67.1 us
    pallas_call x1, Pallas kernels: 68.4 us -> 67.1 us  [local(): pl.pallas_call(functools.partial(kernel, n_mem, n_row, ens_coef), out_sha...]
where the time goes in v5:
time: 69.9 us; the launch traced here: 69.8 us
  Pallas kernels  67.1 us (96%)
  local copies, waits for them, and re-layouts  2.02 us (3%)
    pallas_call x1, Pallas kernels, local(): pl.pallas_call(functools.partial(kernel, n_mem, n_row, ens_coef), out_sha...  67.1 us
    unnamed x3, local copies, waits for them, and re-layouts  2.02 us

profile of v5, /device:TPU:1, one launch (start us, length us, event | category | flops | bytes accessed | tf_op | source)
XLA Modules:
  0.0 69.8 jit_solution(2087936351652805669)
XLA Ops:
  0.6 67.1 %shard_map.76 = (f32[16,2,8,512]{3,2,1,0:T(8,128)S(1)}, f32[2,8,512]{2,1,0:T(8,128)S(1)}, f32[2,8,512]{2,1,0:T(8,128)S(1)}) custom-call(bf16[16,8,16,512]{3,2,1,0:T(8,128)(2,1)} %bitcast.8, f32[2,8,512]{2,1,0:T(8,128)} %bitcast.9, f32[2,8,512]{2,1,0:T(8,128)} %bitcast.10, s32[2,8,512]{2,1,0:T(8,128)} %bitcast.11, s32[2,8,512]{2,1,0:T(8,128)} %index_h.1), custom_call_target="tpu_custom_call" | custom-call | tf_op jit(solution)/shard_map/pallas_call | solution.py:599
  67.7 0.8 %copy.11 = f32[16,2,8,512]{3,2,1,0:T(8,128)} copy(f32[16,2,8,512]{3,2,1,0:T(8,128)S(1)} %get-tuple-element.9) | data formatting | bytes 1048576
  68.5 0.6 copy.12
  69.1 0.6 copy.13

commit v6 on v5

--- a/solution.py
+++ b/solution.py
@@ -24,6 +24,31 @@
     from_left = jnp.where(lane == 0, jnp.concatenate([edge, right[:-1]], 0), right)
     from_right = jnp.where(lane == LANES - 1, jnp.concatenate([left[1:], edge], 0), left)
     return from_left + from_right
+
+
+def pick(tiles, index, source):
+    out = None
+    for t, tile in enumerate(tiles):
+        moved = jnp.take_along_axis(tile, index, axis=1, mode="promise_in_bounds")
+        out = moved if out is None else jnp.where(source == t, moved, out)
+    return out
+
+
+def interleave(tiles):
+    lane = lax.broadcasted_iota(jnp.int32, tiles[0].shape, 1)
+    return [pick(tiles, 4 * lax.rem(lane, 32) + j, lane // 32) for j in range(4)]
+
+
+def in_order(tiles):
+    lane = lax.broadcasted_iota(jnp.int32, tiles[0].shape, 1)
+    return [pick(tiles, 32 * t + lane // 4, lax.rem(lane, 4)) for t in range(4)]
+
+
+def sideways_interleaved(w):
+    lane = lax.broadcasted_iota(jnp.int32, w.shape[1:], 1)
+    before = jnp.where(lane == 0, 0.0, pltpu.roll(w[-1], 1, 1))[None]
+    after = jnp.where(lane == LANES - 1, 0.0, pltpu.roll(w[0], LANES - 1, 1))[None]
+    return jnp.concatenate([before, w[:-1]], 0) + jnp.concatenate([w[1:], after], 0)
 
 
 def kernel(
@@ -60,8 +85,6 @@
         )
         for j in range(tiles)
     ]
-    for load in loads:
-        load.start()
 
     z_hi, y = me_m // 4, lax.rem(me_m, 4)
     x, z_lo, core = me_r // 8, lax.rem(me_r // 2, 4), lax.rem(me_r, 2)
@@ -93,6 +116,9 @@
     @pl.when(has_far)
     def _():
         pl.semaphore_signal(barrier, inc=1, device_id=to(me_m, far), device_id_type=MESH)
+
+    for load in loads:
+        load.start()
 
     def lane_tile(ref, l, j):
         return ref[l, :, j * LANES:(j + 1) * LANES]
@@ -259,7 +285,7 @@
             norm = jnp.zeros((8, LANES), jnp.float32)
             for row in range(lo + 1, hi - 1):
                 u_next, w_next = get(row + 1)
-                out = (w_prev + w_next) + sideways(w_cur) + (u_cur - 4.0 * w_cur)
+                out = (w_prev + w_next) + sideways_interleaved(w_cur) + (u_cur - 4.0 * w_cur)
                 if sweep < SWEEPS - 1:
                     field[l, row, g] = out
                 else:
@@ -283,13 +309,13 @@
             u_prev, u_cur = load(lo), load(lo + 1)
             for row in range(lo + 1, hi - 1):
                 u_next = load(row + 1)
-                out = u_cur + kwide[l, row] * ((u_prev + u_next) + sideways(u_cur) - 4.0 * u_cur)
+                out = u_cur + kwide[l, row] * ((u_prev + u_next) + sideways_interleaved(u_cur) - 4.0 * u_cur)
                 if sweep < SWEEPS - 1:
                     field[l, row, g] = out
                 else:
                     out = out.astype(jnp.bfloat16).astype(jnp.float32)
-                    for j in range(tiles):
-                        spread[l, j, pl.ds((row - rows) * 16 + g * 8, 8), :] = out[j]
+                    for j, tile in enumerate(in_order([out[j] for j in range(tiles)])):
+                        spread[l, j, pl.ds((row - rows) * 16 + g * 8, 8), :] = tile
                 u_prev, u_cur = u_cur, u_next
 
     def diffuse_static(it, l):
@@ -349,8 +375,14 @@
                     for i, value in enumerate(KAPPAS):
                         k = jnp.where(ids == i, value, k)
                     knat[l, j] = k
-                    for row in range(3 * rows):
-                        kwide[l, row, j] = jnp.broadcast_to(k[row:row + 1], (8, LANES))
+            for l in range(2):
+                for third in range(3):
+                    here = slice(third * rows, (third + 1) * rows)
+                    for j, tile in enumerate(interleave([knat[l, j, here] for j in range(tiles)])):
+                        for r in range(rows):
+                            kwide[l, third * rows + r, j] = jnp.broadcast_to(
+                                tile[r:r + 1], (8, LANES)
+                            )
             for load in loads[4:]:
                 load.wait()
             bytes_wait(sent_all.at[0], n_mem - 1, sent_recv)
@@ -368,18 +400,16 @@
                         turned[l, j, k * 8:(k + 1) * 8, :] = total[l * rows:(l + 1) * rows]
 
             for l in range(2):
-                @pl.loop(0, tiles // 2)
-                def _(jj):
-                    for r in range(rows):
-                        pair_of = [
-                            turned[l, jj * 2 + half, pl.ds(g * 64 + r, 8, stride=8), :]
-                            for half in range(2)
-                        ]
-                        for half in range(2):
-                            field[l, rows + r, g, jj * 2 + half] = pair_of[half]
-                        send_back[it, l, g, r, jj] = jnp.concatenate(pair_of, 0).astype(
-                            jnp.bfloat16
-                        )
+                for r in range(rows):
+                    mixed = interleave(
+                        [turned[l, j, pl.ds(g * 64 + r, 8, stride=8), :] for j in range(tiles)]
+                    )
+                    for j in range(tiles):
+                        field[l, rows + r, g, j] = mixed[j]
+                    for jj in range(tiles // 2):
+                        send_back[it, l, g, r, jj] = jnp.concatenate(
+                            mixed[2 * jj:2 * jj + 2], 0
+                        ).astype(jnp.bfloat16)
 
                 row_start(*back_args(it, l, g))
 
@@ -389,9 +419,6 @@
             seen_across().wait_recv()
             for copy in seen_along(partner, 2):
                 copy.start()
-        row_wait(*static_args(it))
-        for l in range(2):
-            diffuse_static(it, l)
 
         def arrive_and_diffuse(l, g):
             row_wait(*back_args(it, l, g))
@@ -435,6 +462,10 @@
             for d in same_rows:
                 part_copy(it, l, d).start()
             arrived[it, l, me_m] = partial[it, l, me_m]
+
+        row_wait(*static_args(it))
+        for l in range(2):
+            diffuse_static(it, l)
 
         curv = jnp.zeros((8, LANES), jnp.float32)
         for l in range(2):
@@ -479,15 +510,15 @@
             bytes_wait(image_all, n_mem - 1, image_recv)
         else:
             for n, out in enumerate((control_o, grad_nat)):
-                @pl.loop(0, tiles)
-                def _(j):
-                    for l in range(2):
-                        for r in range(rows):
-                            for g in range(2):
-                                value = grad[n, l, SWEEPS + r, g, j]
+                @pl.loop(0, 2)
+                def _(l):
+                    for r in range(rows):
+                        for g in range(2):
+                            value = [grad[n, l, SWEEPS + r, g, j] for j in range(tiles)]
+                            for j, tile in enumerate(in_order(value)):
                                 if n == 0:
-                                    value = 0.0 - step_ref[...] * value
-                                spread[l, j, r * 16 + g * 8:r * 16 + g * 8 + 8, :] = value
+                                    tile = 0.0 - step_ref[...] * tile
+                                spread[l, j, r * 16 + g * 8:r * 16 + g * 8 + 8, :] = tile
 
                 for j in range(tiles):
                     for l in range(2):

time: 69.9 us -> 69.6 us (level)
  no operation moved by 1% of the time
where the time goes in v6:
time: 69.6 us; the launch traced here: 69.5 us
  Pallas kernels  66.9 us (96%)
  local copies, waits for them, and re-layouts  2.02 us (3%)
    pallas_call x1, Pallas kernels, local(): pl.pallas_call(functools.partial(kernel, n_mem, n_row, ens_coef), out_sha...  66.9 us
    unnamed x3, local copies, waits for them, and re-layouts  2.02 us

profile of v6, /device:TPU:1, one launch (start us, length us, event | category | flops | bytes accessed | tf_op | source)
XLA Modules:
  0.0 69.5 jit_solution(10790164000727606272)
XLA Ops:
  0.6 66.9 %shard_map.76 = (f32[16,2,8,512]{3,2,1,0:T(8,128)S(1)}, f32[2,8,512]{2,1,0:T(8,128)S(1)}, f32[2,8,512]{2,1,0:T(8,128)S(1)}) custom-call(bf16[16,8,16,512]{3,2,1,0:T(8,128)(2,1)} %bitcast.8, f32[2,8,512]{2,1,0:T(8,128)} %bitcast.9, f32[2,8,512]{2,1,0:T(8,128)} %bitcast.10, s32[2,8,512]{2,1,0:T(8,128)} %bitcast.11, s32[2,8,512]{2,1,0:T(8,128)} %index_h.1), custom_call_target="tpu_custom_call" | custom-call | tf_op jit(solution)/shard_map/pallas_call | solution.py:630
  67.5 0.8 %copy.11 = f32[16,2,8,512]{3,2,1,0:T(8,128)} copy(f32[16,2,8,512]{3,2,1,0:T(8,128)S(1)} %get-tuple-element.9) | data formatting | bytes 1048576
  68.3 0.6 copy.12
  68.9 0.6 copy.13

commit v7 on v5

--- a/solution.py
+++ b/solution.py
@@ -60,8 +60,6 @@
         )
         for j in range(tiles)
     ]
-    for load in loads:
-        load.start()
 
     z_hi, y = me_m // 4, lax.rem(me_m, 4)
     x, z_lo, core = me_r // 8, lax.rem(me_r // 2, 4), lax.rem(me_r, 2)
@@ -93,6 +91,9 @@
     @pl.when(has_far)
     def _():
         pl.semaphore_signal(barrier, inc=1, device_id=to(me_m, far), device_id_type=MESH)
+
+    for load in loads:
+        load.start()
 
     def lane_tile(ref, l, j):
         return ref[l, :, j * LANES:(j + 1) * LANES]
@@ -389,9 +390,6 @@
             seen_across().wait_recv()
             for copy in seen_along(partner, 2):
                 copy.start()
-        row_wait(*static_args(it))
-        for l in range(2):
-            diffuse_static(it, l)
 
         def arrive_and_diffuse(l, g):
             row_wait(*back_args(it, l, g))
@@ -435,6 +433,10 @@
             for d in same_rows:
                 part_copy(it, l, d).start()
             arrived[it, l, me_m] = partial[it, l, me_m]
+
+        row_wait(*static_args(it))
+        for l in range(2):
+            diffuse_static(it, l)
 
         curv = jnp.zeros((8, LANES), jnp.float32)
         for l in range(2):

time: 69.9 us -> 69.8 us (level)
  no operation moved by 1% of the time
where the time goes in v7:
time: 69.8 us; the launch traced here: 69.7 us
  Pallas kernels  67 us (96%)
  local copies, waits for them, and re-layouts  2.02 us (3%)
    pallas_call x1, Pallas kernels, local(): pl.pallas_call(functools.partial(kernel, n_mem, n_row, ens_coef), out_sha...  67 us
    unnamed x3, local copies, waits for them, and re-layouts  2.02 us

profile of v7, /device:TPU:1, one launch (start us, length us, event | category | flops | bytes accessed | tf_op | source)
XLA Modules:
  0.0 69.7 jit_solution(16249281992975405150)
XLA Ops:
  0.6 67.0 %shard_map.76 = (f32[16,2,8,512]{3,2,1,0:T(8,128)S(1)}, f32[2,8,512]{2,1,0:T(8,128)S(1)}, f32[2,8,512]{2,1,0:T(8,128)S(1)}) custom-call(bf16[16,8,16,512]{3,2,1,0:T(8,128)(2,1)} %bitcast.8, f32[2,8,512]{2,1,0:T(8,128)} %bitcast.9, f32[2,8,512]{2,1,0:T(8,128)} %bitcast.10, s32[2,8,512]{2,1,0:T(8,128)} %bitcast.11, s32[2,8,512]{2,1,0:T(8,128)} %index_h.1), custom_call_target="tpu_custom_call" | custom-call | tf_op jit(solution)/shard_map/pallas_call | solution.py:601
  67.6 0.8 %copy.11 = f32[16,2,8,512]{3,2,1,0:T(8,128)} copy(f32[16,2,8,512]{3,2,1,0:T(8,128)S(1)} %get-tuple-element.9) | data formatting | bytes 1048576
  68.4 0.6 copy.12
  69.1 0.6 copy.13
